TPU v7x, 256 devices: a whole 4x4x8 slice. The times are simulated.
256 devices in a mesh: gx: 8 (over z), gy: 8 (over y, core), gz: 4 (over x).
Axes of the slice: x: 4, y: 4, z: 8, core: 2. Of those that a mesh axis runs over, the one named last changes fastest.
Arguments:
- particle_vel: float32 [3, 256, 32, 256], P(None, ('gx', 'gy', 'gz')), may hold values from -6 to 6
- drag_coef: float32 [256, 32, 256], P(('gx', 'gy', 'gz')), may hold values from 1 to 8
- volume: float32 [256, 32, 256], P(('gx', 'gy', 'gz')), may hold values from 0.2 to 3
- stencil_weight: float32 [256, 32, 256], P(('gx', 'gy', 'gz')), may hold values from 0 to 1
- cell_index: int32 [256, 32, 256], P(('gx', 'gy', 'gz')), may hold values from 0 to 131070, as said below
- send_counts: int32 [256, 32], P(('gx', 'gy', 'gz')), may hold values from 1 to 256, as said below
- background_momentum: float32 [3, 256, 256, 512], P(None, 'gx', 'gy', 'gz'), may hold values from -6 to 6
Outputs:
- pressure: float32 [256, 256, 512], P('gx', 'gy', 'gz')
- slot_velocity: float32 [3, 256, 32, 256], P(None, ('gx', 'gy', 'gz'))
Inputs may be any that keep to these rules, and one draw needn't show every extreme that they name: The z coordinate of every cell_index within its block is at most 126, so both stencil cells lie in the destination device's block. `send_counts`: slots of a row below its count are live, the rest empty. Every device holds 256 live slots for its own fluid block, and in every draw some destination device receives 256 live slots from every device of its gx plane.
All inputs are finite; a program needn't handle non-finite values.
Results may differ from a plain program's by a relative error of at most 0.0003.
Values sent between devices are 32-bit elements; how exact they have to be, the bound alone decides.
A program may use at most 64 MiB of HBM per device.

v0:
```python
import jax
import jax.numpy as jnp
from jax import lax
from jax.sharding import PartitionSpec as P

SWEEPS = 4


highest = lax.Precision.HIGHEST


def extended(block, sides, width):
    for axis, dim in sides:
        count = lax.axis_size(axis)
        forward = [(i, i + 1) for i in range(count - 1)]
        backward = [(target, source) for source, target in forward]
        low = lax.ppermute(
            lax.slice_in_dim(block, block.shape[dim] - width, None, axis=dim), axis, forward
        )
        high = lax.ppermute(lax.slice_in_dim(block, 0, width, axis=dim), axis, backward)
        block = jnp.concatenate([low, block, high], axis=dim)
    return block


def shrink(field, margin):
    return field[..., margin:-margin, margin:-margin, margin:-margin]


def neighbour_total(padded, weights):
    plus_x, minus_x, plus_y, minus_y, plus_z, minus_z = weights
    total = plus_x * padded[2:, 1:-1, 1:-1] + minus_x * padded[:-2, 1:-1, 1:-1]
    total = total + plus_y * padded[1:-1, 2:, 1:-1] + minus_y * padded[1:-1, :-2, 1:-1]
    return total + plus_z * padded[1:-1, 1:-1, 2:] + minus_z * padded[1:-1, 1:-1, :-2]


def face_weights(porous):
    centre = porous[1:-1, 1:-1, 1:-1]
    weights = (
        0.5 * (centre + porous[2:, 1:-1, 1:-1]),
        0.5 * (centre + porous[:-2, 1:-1, 1:-1]),
        0.5 * (centre + porous[1:-1, 2:, 1:-1]),
        0.5 * (centre + porous[1:-1, :-2, 1:-1]),
        0.5 * (centre + porous[1:-1, 1:-1, 2:]),
        0.5 * (centre + porous[1:-1, 1:-1, :-2]),
    )
    diagonal = weights[0] + weights[1] + weights[2] + weights[3] + weights[4] + weights[5]
    return (weights, diagonal)


def divergence(moment):
    total = 0.5 * (moment[0, 2:, 1:-1, 1:-1] - moment[0, :-2, 1:-1, 1:-1])
    total = total + 0.5 * (moment[1, 1:-1, 2:, 1:-1] - moment[1, 1:-1, :-2, 1:-1])
    return total + 0.5 * (moment[2, 1:-1, 1:-1, 2:] - moment[2, 1:-1, 1:-1, :-2])


def gradient_of(padded):
    return jnp.stack(
        [
            0.5 * (padded[2:, 1:-1, 1:-1] - padded[:-2, 1:-1, 1:-1]),
            0.5 * (padded[1:-1, 2:, 1:-1] - padded[1:-1, :-2, 1:-1]),
            0.5 * (padded[1:-1, 1:-1, 2:] - padded[1:-1, 1:-1, :-2]),
        ]
    )


def block_rows(group_size, capacity):
    best = 1
    for factor in range(1, group_size + 1):
        if group_size % factor == 0 and factor * capacity <= 2048:
            best = factor
    return best * capacity


def slot_tables(cell_ids, share, columns_all, size_z):
    column = cell_ids // size_z
    height = cell_ids % size_z
    column_hot = (column[:, None] == jnp.arange(columns_all, dtype=jnp.int32)[None, :]).astype(
        jnp.float32
    )
    levels = jnp.arange(size_z, dtype=jnp.int32)[None, :]
    height_weight = share[:, None] * (height[:, None] == levels).astype(jnp.float32) + (
        1.0 - share
    )[:, None] * (height[:, None] + 1 == levels).astype(jnp.float32)
    return (column_hot, height_weight)


def deposit_blocks(carried, cell_ids, share, columns_all, size_z, rows):
    count = cell_ids.shape[0] // rows
    carried_b = carried.reshape(4, count, rows).transpose(1, 0, 2)
    ids_b = cell_ids.reshape(count, rows)
    share_b = share.reshape(count, rows)

    def deposit_step(total, items):
        load, ids, weight = items
        column_hot, height_weight = slot_tables(ids, weight, columns_all, size_z)
        spread = load[:, :, None] * height_weight[None]
        return (total + jnp.einsum("bk,cbz->ckz", column_hot, spread, precision=highest), None)

    start = jnp.zeros((4, columns_all, size_z), jnp.float32)
    total, unused = lax.scan(deposit_step, start, (carried_b, ids_b, share_b))
    return total


def pick_blocks(velocity_cols, cell_ids, share, columns_all, size_z, rows):
    count = cell_ids.shape[0] // rows
    ids_b = cell_ids.reshape(count, rows)
    share_b = share.reshape(count, rows)

    def pick_step(carry, items):
        ids, weight = items
        column_hot, height_weight = slot_tables(ids, weight, columns_all, size_z)
        columns_picked = jnp.einsum("bk,ckz->cbz", column_hot, velocity_cols, precision=highest)
        return (carry, jnp.sum(columns_picked * height_weight[None], axis=2))

    unused, picked = lax.scan(pick_step, jnp.zeros((), jnp.float32), (ids_b, share_b))
    return picked.transpose(1, 0, 2).reshape(3, -1)


def per_device(
    particle_vel, drag_coef, volume, stencil_weight, cell_index, send_counts, background_momentum
):
    group_size = drag_coef.shape[1]
    capacity = drag_coef.shape[2]
    size_x, size_y, size_z = (
        background_momentum.shape[1],
        background_momentum.shape[2],
        background_momentum.shape[3],
    )
    columns_all = size_x * size_y
    rows = block_rows(group_size, capacity)
    slot_pos = jnp.arange(capacity, dtype=jnp.int32)
    alive = (slot_pos[None, :] < send_counts[0][:, None]).astype(jnp.float32)
    strength = drag_coef[0] * alive
    payload = jnp.stack(
        [
            strength * particle_vel[0, 0],
            strength * particle_vel[1, 0],
            strength * particle_vel[2, 0],
            volume[0] * alive,
            stencil_weight[0],
            cell_index[0].astype(jnp.float32),
        ]
    )
    arrived = lax.all_to_all(payload, ("gy", "gz"), split_axis=1, concat_axis=1, tiled=True)
    arrived = arrived.reshape(6, group_size * capacity)
    share = arrived[4]
    cell_ids = arrived[5].astype(jnp.int32)
    carried = arrived[:4]
    deposited = deposit_blocks(carried, cell_ids, share, columns_all, size_z, rows)
    deposited = deposited.reshape(4, size_x, size_y, size_z)
    fields = jnp.concatenate([background_momentum + deposited[:3], deposited[3:]], axis=0)
    padded = extended(fields, (("gx", 1), ("gy", 2), ("gz", 3)), 1)
    porous = 1.0 / (1.0 + padded[3])
    weights, diagonal = face_weights(porous)
    source_div = divergence(padded[:3])
    pressure = (0.0 - source_div) / diagonal
    for sweep_no in range(1, SWEEPS):
        beside_all = extended(pressure, (("gx", 0), ("gy", 1), ("gz", 2)), 1)
        pressure = (neighbour_total(beside_all, weights) - source_div) / diagonal
    pressure_rim = extended(pressure, (("gx", 0), ("gy", 1), ("gz", 2)), 1)
    porosity = shrink(porous, 1)
    momentum = fields[:3]
    fluid_velocity = porosity[None] * (momentum - gradient_of(pressure_rim))
    velocity_cols = fluid_velocity.reshape(3, columns_all, size_z)
    picked = pick_blocks(velocity_cols, cell_ids, share, columns_all, size_z, rows)
    returned = lax.all_to_all(
        picked.reshape(3, group_size, capacity),
        ("gy", "gz"),
        split_axis=1,
        concat_axis=1,
        tiled=True,
    )
    slot_velocity = returned * alive[None]
    return (pressure, slot_velocity.reshape(3, 1, group_size, capacity))


def solution(mesh):
    return jax.shard_map(
        per_device,
        mesh=mesh,
        in_specs=(
            P(None, ("gx", "gy", "gz"), None, None),
            P(("gx", "gy", "gz"), None, None),
            P(("gx", "gy", "gz"), None, None),
            P(("gx", "gy", "gz"), None, None),
            P(("gx", "gy", "gz"), None, None),
            P(("gx", "gy", "gz"), None),
            P(None, "gx", "gy", "gz"),
        ),
        out_specs=(P("gx", "gy", "gz"), P(None, ("gx", "gy", "gz"), None, None)),
        check_vma=False,
    )
```

profile of v0, /device:TPU:129, one launch (start us, length us, event | category | flops | bytes accessed | tf_op | source)
XLA Modules:
  0.0 294.2 jit_solution(11294961227850285346)
XLA Ops:
  5.1 7.8 %all-to-all-start = ((f32[6,32,256]{2,0,1:T(8,128)}), f32[6,32,256]{2,0,1:T(8,128)S(1)}, u32[]{:S(2)}, u32[]{:S(2)}) async-start(f32[6,32,256]{2,0,1:T(8,128)} %stack.20), calls=%async_computation | async-start | bytes 524288 | tf_op jit(solution)/shard_map/all_to_all | solution.py:144
  12.8 8.9 %all-to-all-done = f32[6,32,256]{2,0,1:T(8,128)S(1)} async-done(((f32[6,32,256]{2,0,1:T(8,128)}), f32[6,32,256]{2,0,1:T(8,128)S(1)}, u32[]{:S(2)}, u32[]{:S(2)}) %all-to-all-start) | async-done | bytes 196640 | tf_op jit(solution)/shard_map/all_to_all | solution.py:144
  22.1 34.0 %while.26 = (s32[]{:T(128)}, f32[4,1024,128]{1,2,0:T(8,128)S(1)}, f32[4,4,2048]{2,0,1:T(4,128)S(1)}, s32[4,2048]{1,0:T(4,128)S(1)}, f32[4,2048]{1,0:T(4,128)S(1)}, /*index=5*/s32[]{:T(128)}, s32[]{:T(128)}) while((s32[]{:T(128)}, f32[4,1024,128]{1,2,0:T(8,128)S(1)}, f32[4,4,2048]{2,0,1:T(4,128)S(1)}, s32[4,2048]{1,0:T(4,128)S(1)}, ...), condition=%wide.region_1.2_spmd.clone, body=%wide.region_0.1_spmd.clone.sunk | while | flops 12890449920 | bytes 6578275 | solution.py:100
  22.5 8.1 %bitcast_add_fusion.2 = f32[4,1024,128]{1,2,0:T(8,128)S(1)} fusion(f32[4,1024,128]{1,2,0:T(8,128)S(1)} %get-tuple-element.348, s32[2048]{0:T(1024)S(1)} %get-tuple-element.337, f32[2048,128]{0,1:T(8,128)S(1)} %select_add_fusion.5, f32[4,2048]{1,0:T(4,128)S(1)} %bitcast.91, pred[]{:T(512)S(6)} %compare.27), kind=kOutput, calls=%fused_computation.25.clone.1 | convolution fusion | flops 12889096192 | bytes 5283841 | tf_op jit(solution)/shard_map/while/body/eval_jaxpr/bk,cbz->ckz/dot_general | solution.py:97
  31.0 8.1 %bitcast_add_fusion.2 = f32[4,1024,128]{1,2,0:T(8,128)S(1)} fusion(f32[4,1024,128]{1,2,0:T(8,128)S(1)} %get-tuple-element.348, s32[2048]{0:T(1024)S(1)} %get-tuple-element.337, f32[2048,128]{0,1:T(8,128)S(1)} %select_add_fusion.5, f32[4,2048]{1,0:T(4,128)S(1)} %bitcast.91, pred[]{:T(512)S(6)} %compare.27), kind=kOutput, calls=%fused_computation.25.clone.1 | convolution fusion | flops 12889096192 | bytes 5283841 | tf_op jit(solution)/shard_map/while/body/eval_jaxpr/bk,cbz->ckz/dot_general | solution.py:97
  39.4 8.1 %bitcast_add_fusion.2 = f32[4,1024,128]{1,2,0:T(8,128)S(1)} fusion(f32[4,1024,128]{1,2,0:T(8,128)S(1)} %get-tuple-element.348, s32[2048]{0:T(1024)S(1)} %get-tuple-element.337, f32[2048,128]{0,1:T(8,128)S(1)} %select_add_fusion.5, f32[4,2048]{1,0:T(4,128)S(1)} %bitcast.91, pred[]{:T(512)S(6)} %compare.27), kind=kOutput, calls=%fused_computation.25.clone.1 | convolution fusion | flops 12889096192 | bytes 5283841 | tf_op jit(solution)/shard_map/while/body/eval_jaxpr/bk,cbz->ckz/dot_general | solution.py:97
  47.9 8.1 %bitcast_add_fusion.2 = f32[4,1024,128]{1,2,0:T(8,128)S(1)} fusion(f32[4,1024,128]{1,2,0:T(8,128)S(1)} %get-tuple-element.348, s32[2048]{0:T(1024)S(1)} %get-tuple-element.337, f32[2048,128]{0,1:T(8,128)S(1)} %select_add_fusion.5, f32[4,2048]{1,0:T(4,128)S(1)} %bitcast.91, pred[]{:T(512)S(6)} %compare.27), kind=kOutput, calls=%fused_computation.25.clone.1 | convolution fusion | flops 12889096192 | bytes 5283841 | tf_op jit(solution)/shard_map/while/body/eval_jaxpr/bk,cbz->ckz/dot_general | solution.py:97
  61.2 2.6 collective-permute-start
  63.8 3.8 %collective-permute-start.1 = (f32[4,1,32,128]{3,2,1,0:T(8,128)S(1)}, f32[4,1,32,128]{3,2,1,0:T(8,128)S(1)}, u32[]{:S(2)}, u32[]{:S(2)}) collective-permute-start(f32[4,1,32,128]{3,2,1,0:T(8,128)S(1)} %get-tuple-element.233), channel_id=1, source_target_pairs={{32,0},{64,32},{96,64},{128,96},{160,128},{192,160},{224,192},{33,... | collective-permute-start | bytes 196616 | tf_op jit(solution)/shard_map/ppermute | solution.py:20
  69.1 3.6 %collective-permute-start.2 = (f32[4,34,1,128]{3,2,1,0:T(1,128)S(1)}, f32[4,34,1,128]{3,2,1,0:T(1,128)S(1)}, u32[]{:S(2)}, u32[]{:S(2)}) collective-permute-start(f32[4,34,1,128]{3,2,1,0:T(1,128)S(1)} %get-tuple-element.230), channel_id=1, source_target_pairs={{0,4},{4,8},{8,12},{12,16},{16,20},{20,24},{24,28},{1,5},{5,9},{9,... | collective-permute-start | bytes 208904 | tf_op jit(solution)/shard_map/ppermute | solution.py:17
  72.7 2.1 collective-permute-start.3
  74.8 3.5 %collective-permute-done.3 = f32[4,34,1,128]{3,2,1,0:T(1,128)S(1)} collective-permute-done((f32[4,34,1,128]{3,2,1,0:T(1,128)S(1)}, f32[4,34,1,128]{3,2,1,0:T(1,128)S(1)}, u32[]{:S(2)}, u32[]{:S(2)}) %collective-permute-start.3) | collective-permute-done | bytes 69664 | tf_op jit(solution)/shard_map/ppermute | solution.py:20
  78.9 3.3 %fusion.102 = (f32[4,34,34,1]{3,2,1,0:T(8,128)}, f32[4,34,34,1]{3,2,1,0:T(8,128)}) fusion(f32[4,34,34,128]{3,2,1,0:T(8,128)S(1)} %pad_maximum_fusion), kind=kLoop, calls=%fused_computation.261 | loop fusion | bytes 73984 | tf_op jit(solution)/shard_map/slice | solution.py:18
  82.2 2.8 copy.52
  87.0 2.8 copy.53
  91.2 2.6 copy.54
  94.9 2.6 copy.55
  97.5 2.3 fusion.27
  100.6 3.8 %fusion.89 = (f32[32,32,128]{2,1,0:T(8,128)S(1)}, f32[32,32,128]{2,1,0:T(8,128)}, f32[32,32,128]{2,1,0:T(8,128)}, f32[32,32,128]{2,1,0:T(8,128)}, f32[32,32,128]...) fusion(f32[34,34,130]{2,1,0:T(8,128)S(1)} %fusion.27, ...), kind=kLoop, calls=%fused_computation.228 | loop fusion | flops 6422528 | bytes 10268800 | tf_op jit(solution)/shard_map/div | solution.py:156
  104.4 5.1 %collective-permute-start.6 = (f32[1,32,128]{2,1,0:T(8,128)S(1)}, f32[1,32,128]{2,1,0:T(8,128)S(1)}, u32[]{:S(2)}, u32[]{:S(2)}) collective-permute-start(f32[1,32,128]{2,1,0:T(8,128)S(1)} %get-tuple-element.259), channel_id=1, source_target_pairs={{32,0},{64,32},{96,64},{128,96},{160,128},{192,160},{224,192},{33,... | collective-permute-start | bytes 49160 | tf_op jit(solution)/shard_map/ppermute | solution.py:20
  111.4 3.8 %collective-permute-done.7 = f32[1,32,128]{2,1,0:T(8,128)S(1)} collective-permute-done((f32[1,32,128]{2,1,0:T(8,128)S(1)}, f32[1,32,128]{2,1,0:T(8,128)S(1)}, u32[]{:S(2)}, u32[]{:S(2)}) %collective-permute-start.7) | collective-permute-done | bytes 16416 | tf_op jit(solution)/shard_map/ppermute | solution.py:17
  115.2 2.3 collective-permute-start.8
  117.5 4.7 %collective-permute-start.9 = (f32[34,1,128]{2,1,0:T(1,128)S(1)}, f32[34,1,128]{2,1,0:T(1,128)S(1)}, u32[]{:S(2)}, u32[]{:S(2)}) collective-permute-start(f32[34,1,128]{2,1,0:T(1,128)S(1)} %get-tuple-element.250), channel_id=1, source_target_pairs={{0,4},{4,8},{8,12},{12,16},{16,20},{20,24},{24,28},{1,5},{5,9},{9,... | collective-permute-start | bytes 52232 | tf_op jit(solution)/shard_map/ppermute | solution.py:17
  124.5 2.1 copy.58
  129.9 4.6 %collective-permute-start.11 = (f32[34,34,1]{1,2,0:T(1,128)}, f32[34,34,1]{1,2,0:T(1,128)}, u32[]{:S(2)}, u32[]{:S(2)}) collective-permute-start(f32[34,34,1]{1,2,0:T(1,128)} %copy.60), channel_id=1, source_target_pairs={{0,1},{1,2},{2,3},{4,5},{5,6},{6,7},{8,9},{9,10},{10,11},{12,13},{... | collective-permute-start | bytes 13880 | tf_op jit(solution)/shard_map/ppermute | solution.py:17
  138.4 3.2 %fusion.66 = f32[32,32,128]{2,1,0:T(8,128)S(1)} fusion(f32[32,32,128]{2,1,0:T(8,128)} %get-tuple-element.219, f32[32,32,128]{2,1,0:T(8,128)} %get-tuple-element.218, f32[34,34,1]{2,1,0:T(8,128)} %copy.61, f32[34,1,128]{2,1,0:T(1,128)S(1)} %collective-permute-done.8, f32[34,1,128]{2,1,0:T(1,128)} %copy-done.22, f32[1,32,128]{2,1,0:T(8,128)S(1)} %collective-permute-done.6, ...), kind=kLoop, calls=%fused_computation.157 | loop fusion | flops 4718592 | bytes 4795424 | tf_op jit(solution)/shard_map/div | solution.py:159
  143.6 3.4 %collective-permute-start.13 = (f32[1,32,128]{2,1,0:T(8,128)S(1)}, f32[1,32,128]{2,1,0:T(8,128)S(1)}, u32[]{:S(2)}, u32[]{:S(2)}) collective-permute-start(f32[1,32,128]{2,1,0:T(8,128)S(1)} %get-tuple-element.256), channel_id=1, source_target_pairs={{0,32},{32,64},{64,96},{96,128},{128,160},{160,192},{192,224},{1,3... | collective-permute-start | bytes 49160 | tf_op jit(solution)/shard_map/ppermute | solution.py:17
  146.9 2.3 collective-permute-done.13
  151.2 5.9 %collective-permute-start.15 = (f32[34,1,128]{2,1,0:T(1,128)S(1)}, f32[34,1,128]{2,1,0:T(1,128)S(1)}, u32[]{:S(2)}, u32[]{:S(2)}) collective-permute-start(f32[34,1,128]{2,1,0:T(1,128)S(1)} %get-tuple-element.248), channel_id=1, source_target_pairs={{0,4},{4,8},{8,12},{12,16},{16,20},{20,24},{24,28},{1,5},{5,9},{9,... | collective-permute-start | bytes 52232 | tf_op jit(solution)/shard_map/ppermute | solution.py:17
  159.4 2.1 copy.62
  164.8 4.6 %collective-permute-start.17 = (f32[34,34,1]{1,2,0:T(1,128)}, f32[34,34,1]{1,2,0:T(1,128)}, u32[]{:S(2)}, u32[]{:S(2)}) collective-permute-start(f32[34,34,1]{1,2,0:T(1,128)} %copy.64), channel_id=1, source_target_pairs={{0,1},{1,2},{2,3},{4,5},{5,6},{6,7},{8,9},{9,10},{10,11},{12,13},{... | collective-permute-start | bytes 13880 | tf_op jit(solution)/shard_map/ppermute | solution.py:17
  173.3 3.2 %fusion.53 = f32[32,32,128]{2,1,0:T(8,128)S(1)} fusion(f32[32,32,128]{2,1,0:T(8,128)} %get-tuple-element.219, f32[32,32,128]{2,1,0:T(8,128)} %get-tuple-element.218, f32[34,34,1]{2,1,0:T(8,128)} %copy.65, f32[34,1,128]{2,1,0:T(1,128)S(1)} %collective-permute-done.14, f32[34,1,128]{2,1,0:T(1,128)} %copy-done.23, ...), kind=kLoop, calls=%fused_computation.126 | loop fusion | flops 4718592 | bytes 4795424 | tf_op jit(solution)/shard_map/div | solution.py:159
  178.4 3.4 %collective-permute-start.19 = (f32[1,32,128]{2,1,0:T(8,128)S(1)}, f32[1,32,128]{2,1,0:T(8,128)S(1)}, u32[]{:S(2)}, u32[]{:S(2)}) collective-permute-start(f32[1,32,128]{2,1,0:T(8,128)S(1)} %get-tuple-element.254), channel_id=1, source_target_pairs={{0,32},{32,64},{64,96},{96,128},{128,160},{160,192},{192,224},{1,3... | collective-permute-start | bytes 49160 | tf_op jit(solution)/shard_map/ppermute | solution.py:17
  181.8 2.3 collective-permute-done.19
  186.1 5.9 %collective-permute-start.21 = (f32[34,1,128]{2,1,0:T(1,128)S(1)}, f32[34,1,128]{2,1,0:T(1,128)S(1)}, u32[]{:S(2)}, u32[]{:S(2)}) collective-permute-start(f32[34,1,128]{2,1,0:T(1,128)S(1)} %get-tuple-element.246), channel_id=1, source_target_pairs={{0,4},{4,8},{8,12},{12,16},{16,20},{20,24},{24,28},{1,5},{5,9},{9,... | collective-permute-start | bytes 52232 | tf_op jit(solution)/shard_map/ppermute | solution.py:17
  198.4 4.2 %collective-permute-start.23 = (f32[34,34,1]{1,2,0:T(1,128)S(1)}, f32[34,34,1]{1,2,0:T(1,128)S(1)}, u32[]{:S(2)}, u32[]{:S(2)}) collective-permute-start(f32[34,34,1]{1,2,0:T(1,128)S(1)} %copy.68), channel_id=1, source_target_pairs={{0,1},{1,2},{2,3},{4,5},{5,6},{6,7},{8,9},{9,10},{10,11},{12,13},{... | collective-permute-start | bytes 13880 | tf_op jit(solution)/shard_map/ppermute | solution.py:17
  205.1 4.4 %fusion.40 = f32[32,32,128]{2,1,0:T(8,128)S(1)} fusion(f32[32,32,128]{2,1,0:T(8,128)} %get-tuple-element.219, f32[32,32,128]{2,1,0:T(8,128)} %get-tuple-element.218, f32[34,34,1]{2,1,0:T(8,128)} %copy.69, f32[34,1,128]{2,1,0:T(1,128)S(1)} %collective-permute-done.20, f32[34,1,128]{2,1,0:T(1,128)} %copy-done.21, ...), kind=kLoop, calls=%fused_computation.95 | loop fusion | flops 4718592 | bytes 4795424 | tf_op jit(solution)/shard_map/div | solution.py:159
  211.5 3.4 %collective-permute-start.25 = (f32[1,32,128]{2,1,0:T(8,128)S(1)}, f32[1,32,128]{2,1,0:T(8,128)S(1)}, u32[]{:S(2)}, u32[]{:S(2)}) collective-permute-start(f32[1,32,128]{2,1,0:T(8,128)S(1)} %get-tuple-element.252), channel_id=1, source_target_pairs={{0,32},{32,64},{64,96},{96,128},{128,160},{160,192},{192,224},{1,3... | collective-permute-start | bytes 49160 | tf_op jit(solution)/shard_map/ppermute | solution.py:17
  214.9 2.3 collective-permute-done.25
  219.8 5.9 %collective-permute-start.27 = (f32[34,1,128]{2,1,0:T(1,128)}, f32[34,1,128]{2,1,0:T(1,128)}, u32[]{:S(2)}, u32[]{:S(2)}) collective-permute-start(f32[34,1,128]{2,1,0:T(1,128)} %get-tuple-element.244), channel_id=1, source_target_pairs={{0,4},{4,8},{8,12},{12,16},{16,20},{20,24},{24,28},{1,5},{5,9},{9,... | collective-permute-start | bytes 52232 | tf_op jit(solution)/shard_map/ppermute | solution.py:17
  232.4 5.1 %collective-permute-start.29 = (f32[34,34,1]{1,0,2:T(8,128)}, f32[34,34,1]{1,0,2:T(8,128)}, u32[]{:S(2)}, u32[]{:S(2)}) collective-permute-start(f32[34,34,1]{1,0,2:T(8,128)} %copy.72), channel_id=1, source_target_pairs={{0,1},{1,2},{2,3},{4,5},{5,6},{6,7},{8,9},{9,10},{10,11},{12,13},{... | collective-permute-start | bytes 13880 | tf_op jit(solution)/shard_map/ppermute | solution.py:17
  244.0 33.4 %while.25 = (s32[]{:T(128)}, f32[4,3,2048]{2,1,0:T(4,128)}, s32[4,2048]{1,0:T(4,128)}, f32[3,1024,128]{1,2,0:T(8,128)S(1)}, f32[4,2048]{1,0:T(4,128)}, /*index=5*/s32[]{:T(128)}) while((s32[]{:T(128)}, f32[4,3,2048]{2,1,0:T(4,128)}, s32[4,2048]{1,0:T(4,128)}, f32[3,1024,128]{1,2,0:T(8,128)S(1)}, f32[4,2048]{1,0:T(4,128)}, ...), condition=%wide.region_4.5_spmd, body=%wide.region_2.4_spmd.sunk | while | flops 9668694016 | bytes 10166861 | solution.py:115
  245.7 5.6 %fusion.118 = f32[2048,384]{0,1:S(1)} fusion(f32[1024,384]{0,1:T(8,128)S(1)} %bitcast.90, s32[2048]{0:T(1024)S(1)} %get-tuple-element.329), kind=kOutput, calls=%fused_computation.1.clone.1 | convolution fusion | flops 9665773568 | bytes 4726784 | tf_op jit(solution)/shard_map/while
  254.1 5.6 %fusion.118 = f32[2048,384]{0,1:S(1)} fusion(f32[1024,384]{0,1:T(8,128)S(1)} %bitcast.90, s32[2048]{0:T(1024)S(1)} %get-tuple-element.329), kind=kOutput, calls=%fused_computation.1.clone.1 | convolution fusion | flops 9665773568 | bytes 4726784 | tf_op jit(solution)/shard_map/while
  262.5 5.6 %fusion.118 = f32[2048,384]{0,1:S(1)} fusion(f32[1024,384]{0,1:T(8,128)S(1)} %bitcast.90, s32[2048]{0:T(1024)S(1)} %get-tuple-element.329), kind=kOutput, calls=%fused_computation.1.clone.1 | convolution fusion | flops 9665773568 | bytes 4726784 | tf_op jit(solution)/shard_map/while
  270.8 5.6 %fusion.118 = f32[2048,384]{0,1:S(1)} fusion(f32[1024,384]{0,1:T(8,128)S(1)} %bitcast.90, s32[2048]{0:T(1024)S(1)} %get-tuple-element.329), kind=kOutput, calls=%fused_computation.1.clone.1 | convolution fusion | flops 9665773568 | bytes 4726784 | tf_op jit(solution)/shard_map/while
  277.4 8.5 %all-to-all-start.1 = ((f32[3,32,256]{2,0,1:T(4,128)}), f32[3,32,256]{2,0,1:T(4,128)S(1)}, u32[]{:S(2)}, u32[]{:S(2)}) async-start(f32[3,32,256]{2,0,1:T(4,128)} %bitcast.21), calls=%async_computation.1 | async-start | bytes 262144 | tf_op jit(solution)/shard_map/all_to_all | solution.py:166
  286.0 7.5 %all-to-all-done.1 = f32[3,32,256]{2,0,1:T(4,128)S(1)} async-done(((f32[3,32,256]{2,0,1:T(4,128)}), f32[3,32,256]{2,0,1:T(4,128)S(1)}, u32[]{:S(2)}, u32[]{:S(2)}) %all-to-all-start.1) | async-done | bytes 98336 | tf_op jit(solution)/shard_map/all_to_all | solution.py:166
  (205 shorter events, 85.0 us)
Async XLA Ops:
  5.1 16.7 %all-to-all-start = ((f32[6,32,256]{2,0,1:T(8,128)}), f32[6,32,256]{2,0,1:T(8,128)S(1)}, u32[]{:S(2)}, u32[]{:S(2)}) async-start(f32[6,32,256]{2,0,1:T(8,128)} %stack.20), calls=%async_computation | async-start | bytes 524288 | tf_op jit(solution)/shard_map/all_to_all | solution.py:144
  57.4 2.0 copy-start.20
  61.2 6.6 %collective-permute-start = (f32[4,1,32,128]{3,2,1,0:T(8,128)S(1)}, f32[4,1,32,128]{3,2,1,0:T(8,128)S(1)}, u32[]{:S(2)}, u32[]{:S(2)}) collective-permute-start(f32[4,1,32,128]{3,2,1,0:T(8,128)S(1)} %get-tuple-element.232), channel_id=1, source_target_pairs={{0,32},{32,64},{64,96},{96,128},{128,160},{160,192},{192,224},{1,3... | collective-permute-start | bytes 196616 | tf_op jit(solution)/shard_map/ppermute | solution.py:17
  63.8 5.2 %collective-permute-start.1 = (f32[4,1,32,128]{3,2,1,0:T(8,128)S(1)}, f32[4,1,32,128]{3,2,1,0:T(8,128)S(1)}, u32[]{:S(2)}, u32[]{:S(2)}) collective-permute-start(f32[4,1,32,128]{3,2,1,0:T(8,128)S(1)} %get-tuple-element.233), channel_id=1, source_target_pairs={{32,0},{64,32},{96,64},{128,96},{160,128},{192,160},{224,192},{33,... | collective-permute-start | bytes 196616 | tf_op jit(solution)/shard_map/ppermute | solution.py:20
  69.0 9.7 %copy-start.13 = (f32[4,1,32,128]{3,2,1,0:T(8,128)}, f32[4,1,32,128]{3,2,1,0:T(8,128)S(1)}, u32[]{:S(2)}) copy-start(f32[4,1,32,128]{3,2,1,0:T(8,128)S(1)} %collective-permute-done.1) | copy-start | bytes 196612
  69.1 5.7 %collective-permute-start.2 = (f32[4,34,1,128]{3,2,1,0:T(1,128)S(1)}, f32[4,34,1,128]{3,2,1,0:T(1,128)S(1)}, u32[]{:S(2)}, u32[]{:S(2)}) collective-permute-start(f32[4,34,1,128]{3,2,1,0:T(1,128)S(1)} %get-tuple-element.230), channel_id=1, source_target_pairs={{0,4},{4,8},{8,12},{12,16},{16,20},{20,24},{24,28},{1,5},{5,9},{9,... | collective-permute-start | bytes 208904 | tf_op jit(solution)/shard_map/ppermute | solution.py:17
  72.7 5.6 %collective-permute-start.3 = (f32[4,34,1,128]{3,2,1,0:T(1,128)S(1)}, f32[4,34,1,128]{3,2,1,0:T(1,128)S(1)}, u32[]{:S(2)}, u32[]{:S(2)}) collective-permute-start(f32[4,34,1,128]{3,2,1,0:T(1,128)S(1)} %get-tuple-element.231), channel_id=1, source_target_pairs={{4,0},{8,4},{12,8},{16,12},{20,16},{24,20},{28,24},{5,1},{9,5},{13... | collective-permute-start | bytes 208904 | tf_op jit(solution)/shard_map/ppermute | solution.py:20
  74.8 4.0 %copy-start.15 = (f32[4,34,1,128]{3,2,1,0:T(1,128)}, f32[4,34,1,128]{3,2,1,0:T(1,128)S(1)}, u32[]{:S(2)}) copy-start(f32[4,34,1,128]{3,2,1,0:T(1,128)S(1)} %collective-permute-done.2) | copy-start | bytes 208900
  85.0 6.1 %collective-permute-start.4 = (f32[4,34,34,1]{2,0,3,1:T(4,128)S(1)}, f32[4,34,34,1]{2,0,3,1:T(4,128)S(1)}, u32[]{:S(2)}, u32[]{:S(2)}) collective-permute-start(f32[4,34,34,1]{2,0,3,1:T(4,128)S(1)} %copy.52), channel_id=1, source_target_pairs={{0,1},{1,2},{2,3},{4,5},{5,6},{6,7},{8,9},{9,10},{10,11},{12,13},{... | collective-permute-start | bytes 55496 | tf_op jit(solution)/shard_map/ppermute | solution.py:17
  89.9 5.1 %collective-permute-start.5 = (f32[4,34,34,1]{2,0,3,1:T(4,128)S(1)}, f32[4,34,34,1]{2,0,3,1:T(4,128)S(1)}, u32[]{:S(2)}, u32[]{:S(2)}) collective-permute-start(f32[4,34,34,1]{2,0,3,1:T(4,128)S(1)} %copy.53), channel_id=1, source_target_pairs={{1,0},{2,1},{3,2},{5,4},{6,5},{7,6},{9,8},{10,9},{11,10},{13,12},{... | collective-permute-start | bytes 55496 | tf_op jit(solution)/shard_map/ppermute | solution.py:20
  97.5 2.3 copy-start
  97.5 3.1 %copy-start.1 = (f32[4,34,34,1]{3,2,1,0:T(8,128)S(1)}, f32[4,34,34,1]{3,2,1,0:T(8,128)}, u32[]{:S(2)}) copy-start(f32[4,34,34,1]{3,2,1,0:T(8,128)} %copy.55) | copy-start | bytes 55492
  97.5 3.1 %copy-start.14 = (f32[4,1,32,128]{3,2,1,0:T(8,128)S(1)}, f32[4,1,32,128]{3,2,1,0:T(8,128)}, u32[]{:S(2)}) copy-start(f32[4,1,32,128]{3,2,1,0:T(8,128)} %copy-done.13) | copy-start | bytes 196612
  97.5 3.1 %copy-start.16 = (f32[4,34,1,128]{3,2,1,0:T(1,128)S(1)}, f32[4,34,1,128]{3,2,1,0:T(1,128)}, u32[]{:S(2)}) copy-start(f32[4,34,1,128]{3,2,1,0:T(1,128)} %copy-done.15) | copy-start | bytes 208900
  97.5 3.1 %copy-start.18 = (f32[4,34,1,128]{3,2,1,0:T(1,128)S(1)}, f32[4,34,1,128]{3,2,1,0:T(1,128)}, u32[]{:S(2)}) copy-start(f32[4,34,1,128]{3,2,1,0:T(1,128)} %copy-done.17) | copy-start | bytes 208900
  104.4 20.1 %copy-start.3 = (f32[32,32,128]{2,1,0:T(8,128)}, f32[32,32,128]{2,1,0:T(8,128)S(1)}, u32[]{:S(2)}) copy-start(f32[32,32,128]{2,1,0:T(8,128)S(1)} %get-tuple-element.212) | copy-start | bytes 1572868
  104.4 7.0 %collective-permute-start.6 = (f32[1,32,128]{2,1,0:T(8,128)S(1)}, f32[1,32,128]{2,1,0:T(8,128)S(1)}, u32[]{:S(2)}, u32[]{:S(2)}) collective-permute-start(f32[1,32,128]{2,1,0:T(8,128)S(1)} %get-tuple-element.259), channel_id=1, source_target_pairs={{32,0},{64,32},{96,64},{128,96},{160,128},{192,160},{224,192},{33,... | collective-permute-start | bytes 49160 | tf_op jit(solution)/shard_map/ppermute | solution.py:20
  109.5 5.7 %collective-permute-start.7 = (f32[1,32,128]{2,1,0:T(8,128)S(1)}, f32[1,32,128]{2,1,0:T(8,128)S(1)}, u32[]{:S(2)}, u32[]{:S(2)}) collective-permute-start(f32[1,32,128]{2,1,0:T(8,128)S(1)} %get-tuple-element.258), channel_id=1, source_target_pairs={{0,32},{32,64},{64,96},{96,128},{128,160},{160,192},{192,224},{1,3... | collective-permute-start | bytes 49160 | tf_op jit(solution)/shard_map/ppermute | solution.py:17
  115.2 7.1 %collective-permute-start.8 = (f32[34,1,128]{2,1,0:T(1,128)S(1)}, f32[34,1,128]{2,1,0:T(1,128)S(1)}, u32[]{:S(2)}, u32[]{:S(2)}) collective-permute-start(f32[34,1,128]{2,1,0:T(1,128)S(1)} %get-tuple-element.251), channel_id=1, source_target_pairs={{4,0},{8,4},{12,8},{16,12},{20,16},{24,20},{28,24},{5,1},{9,5},{13... | collective-permute-start | bytes 52232 | tf_op jit(solution)/shard_map/ppermute | solution.py:20
  117.5 5.6 %collective-permute-start.9 = (f32[34,1,128]{2,1,0:T(1,128)S(1)}, f32[34,1,128]{2,1,0:T(1,128)S(1)}, u32[]{:S(2)}, u32[]{:S(2)}) collective-permute-start(f32[34,1,128]{2,1,0:T(1,128)S(1)} %get-tuple-element.250), channel_id=1, source_target_pairs={{0,4},{4,8},{8,12},{12,16},{16,20},{20,24},{24,28},{1,5},{5,9},{9,... | collective-permute-start | bytes 52232 | tf_op jit(solution)/shard_map/ppermute | solution.py:17
  124.5 13.9 %copy-start.4 = (f32[32,32,128]{2,1,0:T(8,128)S(1)}, f32[32,32,128]{2,1,0:T(8,128)}, u32[]{:S(2)}) copy-start(f32[32,32,128]{2,1,0:T(8,128)} %copy-done.3) | copy-start | bytes 1572868
  126.6 7.9 %collective-permute-start.10 = (f32[34,34,1]{1,2,0:T(1,128)}, f32[34,34,1]{1,2,0:T(1,128)}, u32[]{:S(2)}, u32[]{:S(2)}) collective-permute-start(f32[34,34,1]{1,2,0:T(1,128)} %copy.58), channel_id=1, source_target_pairs={{1,0},{2,1},{3,2},{5,4},{6,5},{7,6},{9,8},{10,9},{11,10},{13,12},{... | collective-permute-start | bytes 13880 | tf_op jit(solution)/shard_map/ppermute | solution.py:20
  129.9 6.5 %collective-permute-start.11 = (f32[34,34,1]{1,2,0:T(1,128)}, f32[34,34,1]{1,2,0:T(1,128)}, u32[]{:S(2)}, u32[]{:S(2)}) collective-permute-start(f32[34,34,1]{1,2,0:T(1,128)} %copy.60), channel_id=1, source_target_pairs={{0,1},{1,2},{2,3},{4,5},{5,6},{6,7},{8,9},{9,10},{10,11},{12,13},{... | collective-permute-start | bytes 13880 | tf_op jit(solution)/shard_map/ppermute | solution.py:17
  141.6 17.8 %copy-start.6 = (f32[32,32,128]{2,1,0:T(8,128)}, f32[32,32,128]{2,1,0:T(8,128)S(1)}, u32[]{:S(2)}) copy-start(f32[32,32,128]{2,1,0:T(8,128)S(1)} %fusion.66) | copy-start | bytes 1572868
  141.6 5.3 %collective-permute-start.12 = (f32[1,32,128]{2,1,0:T(8,128)S(1)}, f32[1,32,128]{2,1,0:T(8,128)S(1)}, u32[]{:S(2)}, u32[]{:S(2)}) collective-permute-start(f32[1,32,128]{2,1,0:T(8,128)S(1)} %get-tuple-element.257), channel_id=1, source_target_pairs={{32,0},{64,32},{96,64},{128,96},{160,128},{192,160},{224,192},{33,... | collective-permute-start | bytes 49160 | tf_op jit(solution)/shard_map/ppermute | solution.py:20
  143.6 5.7 %collective-permute-start.13 = (f32[1,32,128]{2,1,0:T(8,128)S(1)}, f32[1,32,128]{2,1,0:T(8,128)S(1)}, u32[]{:S(2)}, u32[]{:S(2)}) collective-permute-start(f32[1,32,128]{2,1,0:T(8,128)S(1)} %get-tuple-element.256), channel_id=1, source_target_pairs={{0,32},{32,64},{64,96},{96,128},{128,160},{160,192},{192,224},{1,3... | collective-permute-start | bytes 49160 | tf_op jit(solution)/shard_map/ppermute | solution.py:17
  149.3 7.9 %collective-permute-start.14 = (f32[34,1,128]{2,1,0:T(1,128)S(1)}, f32[34,1,128]{2,1,0:T(1,128)S(1)}, u32[]{:S(2)}, u32[]{:S(2)}) collective-permute-start(f32[34,1,128]{2,1,0:T(1,128)S(1)} %get-tuple-element.249), channel_id=1, source_target_pairs={{4,0},{8,4},{12,8},{16,12},{20,16},{24,20},{28,24},{5,1},{9,5},{13... | collective-permute-start | bytes 52232 | tf_op jit(solution)/shard_map/ppermute | solution.py:20
  151.2 6.8 %collective-permute-start.15 = (f32[34,1,128]{2,1,0:T(1,128)S(1)}, f32[34,1,128]{2,1,0:T(1,128)S(1)}, u32[]{:S(2)}, u32[]{:S(2)}) collective-permute-start(f32[34,1,128]{2,1,0:T(1,128)S(1)} %get-tuple-element.248), channel_id=1, source_target_pairs={{0,4},{4,8},{8,12},{12,16},{16,20},{20,24},{24,28},{1,5},{5,9},{9,... | collective-permute-start | bytes 52232 | tf_op jit(solution)/shard_map/ppermute | solution.py:17
  159.4 13.9 %copy-start.7 = (f32[32,32,128]{2,1,0:T(8,128)S(1)}, f32[32,32,128]{2,1,0:T(8,128)}, u32[]{:S(2)}) copy-start(f32[32,32,128]{2,1,0:T(8,128)} %copy-done.6) | copy-start | bytes 1572868
  161.5 7.9 %collective-permute-start.16 = (f32[34,34,1]{1,2,0:T(1,128)}, f32[34,34,1]{1,2,0:T(1,128)}, u32[]{:S(2)}, u32[]{:S(2)}) collective-permute-start(f32[34,34,1]{1,2,0:T(1,128)} %copy.62), channel_id=1, source_target_pairs={{1,0},{2,1},{3,2},{5,4},{6,5},{7,6},{9,8},{10,9},{11,10},{13,12},{... | collective-permute-start | bytes 13880 | tf_op jit(solution)/shard_map/ppermute | solution.py:20
  164.8 6.5 %collective-permute-start.17 = (f32[34,34,1]{1,2,0:T(1,128)}, f32[34,34,1]{1,2,0:T(1,128)}, u32[]{:S(2)}, u32[]{:S(2)}) collective-permute-start(f32[34,34,1]{1,2,0:T(1,128)} %copy.64), channel_id=1, source_target_pairs={{0,1},{1,2},{2,3},{4,5},{5,6},{6,7},{8,9},{9,10},{10,11},{12,13},{... | collective-permute-start | bytes 13880 | tf_op jit(solution)/shard_map/ppermute | solution.py:17
  176.5 17.8 %copy-start.5 = (f32[32,32,128]{2,1,0:T(8,128)}, f32[32,32,128]{2,1,0:T(8,128)S(1)}, u32[]{:S(2)}) copy-start(f32[32,32,128]{2,1,0:T(8,128)S(1)} %fusion.53) | copy-start | bytes 1572868
  176.5 5.3 %collective-permute-start.18 = (f32[1,32,128]{2,1,0:T(8,128)S(1)}, f32[1,32,128]{2,1,0:T(8,128)S(1)}, u32[]{:S(2)}, u32[]{:S(2)}) collective-permute-start(f32[1,32,128]{2,1,0:T(8,128)S(1)} %get-tuple-element.255), channel_id=1, source_target_pairs={{32,0},{64,32},{96,64},{128,96},{160,128},{192,160},{224,192},{33,... | collective-permute-start | bytes 49160 | tf_op jit(solution)/shard_map/ppermute | solution.py:20
  178.4 5.7 %collective-permute-start.19 = (f32[1,32,128]{2,1,0:T(8,128)S(1)}, f32[1,32,128]{2,1,0:T(8,128)S(1)}, u32[]{:S(2)}, u32[]{:S(2)}) collective-permute-start(f32[1,32,128]{2,1,0:T(8,128)S(1)} %get-tuple-element.254), channel_id=1, source_target_pairs={{0,32},{32,64},{64,96},{96,128},{128,160},{160,192},{192,224},{1,3... | collective-permute-start | bytes 49160 | tf_op jit(solution)/shard_map/ppermute | solution.py:17
  184.2 7.9 %collective-permute-start.20 = (f32[34,1,128]{2,1,0:T(1,128)S(1)}, f32[34,1,128]{2,1,0:T(1,128)S(1)}, u32[]{:S(2)}, u32[]{:S(2)}) collective-permute-start(f32[34,1,128]{2,1,0:T(1,128)S(1)} %get-tuple-element.247), channel_id=1, source_target_pairs={{4,0},{8,4},{12,8},{16,12},{20,16},{24,20},{28,24},{5,1},{9,5},{13... | collective-permute-start | bytes 52232 | tf_op jit(solution)/shard_map/ppermute | solution.py:20
  186.1 6.8 %collective-permute-start.21 = (f32[34,1,128]{2,1,0:T(1,128)S(1)}, f32[34,1,128]{2,1,0:T(1,128)S(1)}, u32[]{:S(2)}, u32[]{:S(2)}) collective-permute-start(f32[34,1,128]{2,1,0:T(1,128)S(1)} %get-tuple-element.246), channel_id=1, source_target_pairs={{0,4},{4,8},{8,12},{12,16},{16,20},{20,24},{24,28},{1,5},{5,9},{9,... | collective-permute-start | bytes 52232 | tf_op jit(solution)/shard_map/ppermute | solution.py:17
  192.9 2.9 copy-start.21
  195.7 6.9 %collective-permute-start.22 = (f32[34,34,1]{1,2,0:T(1,128)S(1)}, f32[34,34,1]{1,2,0:T(1,128)S(1)}, u32[]{:S(2)}, u32[]{:S(2)}) collective-permute-start(f32[34,34,1]{1,2,0:T(1,128)S(1)} %copy.66), channel_id=1, source_target_pairs={{1,0},{2,1},{3,2},{5,4},{6,5},{7,6},{9,8},{10,9},{11,10},{13,12},{... | collective-permute-start | bytes 13880 | tf_op jit(solution)/shard_map/ppermute | solution.py:20
  198.4 5.4 %collective-permute-start.23 = (f32[34,34,1]{1,2,0:T(1,128)S(1)}, f32[34,34,1]{1,2,0:T(1,128)S(1)}, u32[]{:S(2)}, u32[]{:S(2)}) collective-permute-start(f32[34,34,1]{1,2,0:T(1,128)S(1)} %copy.68), channel_id=1, source_target_pairs={{0,1},{1,2},{2,3},{4,5},{5,6},{6,7},{8,9},{9,10},{10,11},{12,13},{... | collective-permute-start | bytes 13880 | tf_op jit(solution)/shard_map/ppermute | solution.py:17
  209.6 32.0 %copy-start.2 = (f32[32,32,128]{2,1,0:T(8,128)}, f32[32,32,128]{2,1,0:T(8,128)S(1)}, u32[]{:S(2)}) copy-start(f32[32,32,128]{2,1,0:T(8,128)S(1)} %fusion.40) | copy-start | bytes 1572868
  209.6 5.3 %collective-permute-start.24 = (f32[1,32,128]{2,1,0:T(8,128)S(1)}, f32[1,32,128]{2,1,0:T(8,128)S(1)}, u32[]{:S(2)}, u32[]{:S(2)}) collective-permute-start(f32[1,32,128]{2,1,0:T(8,128)S(1)} %get-tuple-element.253), channel_id=1, source_target_pairs={{32,0},{64,32},{96,64},{128,96},{160,128},{192,160},{224,192},{33,... | collective-permute-start | bytes 49160 | tf_op jit(solution)/shard_map/ppermute | solution.py:20
  211.5 5.7 %collective-permute-start.25 = (f32[1,32,128]{2,1,0:T(8,128)S(1)}, f32[1,32,128]{2,1,0:T(8,128)S(1)}, u32[]{:S(2)}, u32[]{:S(2)}) collective-permute-start(f32[1,32,128]{2,1,0:T(8,128)S(1)} %get-tuple-element.252), channel_id=1, source_target_pairs={{0,32},{32,64},{64,96},{96,128},{128,160},{160,192},{192,224},{1,3... | collective-permute-start | bytes 49160 | tf_op jit(solution)/shard_map/ppermute | solution.py:17
  217.9 8.9 %collective-permute-start.26 = (f32[34,1,128]{2,1,0:T(1,128)}, f32[34,1,128]{2,1,0:T(1,128)S(1)}, u32[]{:S(2)}, u32[]{:S(2)}) collective-permute-start(f32[34,1,128]{2,1,0:T(1,128)} %get-tuple-element.245), channel_id=1, source_target_pairs={{4,0},{8,4},{12,8},{16,12},{20,16},{24,20},{28,24},{5,1},{9,5},{13... | collective-permute-start | bytes 52232 | tf_op jit(solution)/shard_map/ppermute | solution.py:20
  219.8 7.0 %collective-permute-start.27 = (f32[34,1,128]{2,1,0:T(1,128)}, f32[34,1,128]{2,1,0:T(1,128)}, u32[]{:S(2)}, u32[]{:S(2)}) collective-permute-start(f32[34,1,128]{2,1,0:T(1,128)} %get-tuple-element.244), channel_id=1, source_target_pairs={{0,4},{4,8},{8,12},{12,16},{16,20},{20,24},{24,28},{1,5},{5,9},{9,... | collective-permute-start | bytes 52232 | tf_op jit(solution)/shard_map/ppermute | solution.py:17
  230.1 9.3 %collective-permute-start.28 = (f32[34,34,1]{1,0,2:T(8,128)S(1)}, f32[34,34,1]{1,0,2:T(8,128)}, u32[]{:S(2)}, u32[]{:S(2)}) collective-permute-start(f32[34,34,1]{1,0,2:T(8,128)S(1)} %copy.70), channel_id=1, source_target_pairs={{1,0},{2,1},{3,2},{5,4},{6,5},{7,6},{9,8},{10,9},{11,10},{13,12},{... | collective-permute-start | bytes 13880 | tf_op jit(solution)/shard_map/ppermute | solution.py:20
  232.4 8.1 %collective-permute-start.29 = (f32[34,34,1]{1,0,2:T(8,128)}, f32[34,34,1]{1,0,2:T(8,128)}, u32[]{:S(2)}, u32[]{:S(2)}) collective-permute-start(f32[34,34,1]{1,0,2:T(8,128)} %copy.72), channel_id=1, source_target_pairs={{0,1},{1,2},{2,3},{4,5},{5,6},{6,7},{8,9},{9,10},{10,11},{12,13},{... | collective-permute-start | bytes 13880 | tf_op jit(solution)/shard_map/ppermute | solution.py:17
  244.0 42.0 %copy-start.24 = (s32[1,32]{1,0:T(1,128)S(1)}, s32[1,32]{1,0:T(1,128)}, u32[]{:S(2)}) copy-start(s32[1,32]{1,0:T(1,128)} %param.16) | copy-start | bytes 388
  277.4 16.1 %all-to-all-start.1 = ((f32[3,32,256]{2,0,1:T(4,128)}), f32[3,32,256]{2,0,1:T(4,128)S(1)}, u32[]{:S(2)}, u32[]{:S(2)}) async-start(f32[3,32,256]{2,0,1:T(4,128)} %bitcast.21), calls=%async_computation.1 | async-start | bytes 262144 | tf_op jit(solution)/shard_map/all_to_all | solution.py:166
  (9 other events, 12.4 us)
where the time goes:
time: 297 us; the launch traced here: 294 us
  starting transfers between devices  109 us (37%)
  local copies, waits for them, and re-layouts  64.7 us (22%)
  matrix products  54.8 us (18%)
  waiting for transfers between devices  35.6 us (12%)
  other arithmetic  28.6 us (10%)
    ppermute x15, starting transfers between devices, extended(): lax.ppermute(lax.slice_in_dim(block, block.shape[dim] - width, None, axis...  61.2 us
    dot_general x4, matrix products, deposit_step(): jnp.einsum('bk,cbz->ckz', column_hot, spread, precision=highest)  32.6 us
    ppermute x15, starting transfers between devices, extended(): lax.ppermute(lax.slice_in_dim(block, 0, width, axis=dim), axis, backward)  31.2 us
    while x4, matrix products  22.2 us
    slice x9, local copies, waits for them, and re-layouts, extended(): lax.slice_in_dim(block, 0, width, axis=dim)  14.9 us
    ppermute x15, waiting for transfers between devices, extended(): lax.ppermute(lax.slice_in_dim(block, block.shape[dim] - width, None, axis...  13.4 us
    slice x10, local copies, waits for them, and re-layouts, extended(): lax.slice_in_dim(block, block.shape[dim] - width, None, axis=dim)  12.6 us
    div x3, other arithmetic, per_device(): pressure = (neighbour_total(beside_all, weights) - source_div) / diagonal  10.8 us
  transfers between devices with their start and end apart: 32, of which 13 were waited for; matrix products, arithmetic and copies ran while one was open for 7% of the time, Pallas kernels for 0%

commit v1 on v0

v1 whole, which is shorter than its diff:
```python
import functools

import jax
import jax.numpy as jnp
from jax import lax
from jax.experimental import pallas as pl
from jax.experimental.pallas import tpu as pltpu
from jax.sharding import PartitionSpec as P

SWEEPS = 4
F32 = jnp.float32
BF16 = jnp.bfloat16
MESH = pl.DeviceIdType.MESH
LANES = 128
STEP = 4


def iota(shape, dim):
    return lax.broadcasted_iota(jnp.int32, shape, dim)


def dot(lhs, rhs, contract):
    return lax.dot_general(lhs, rhs, (contract, ((), ())), preferred_element_type=F32)


def split(value):
    high = value.astype(BF16)
    return high.astype(F32), value - high.astype(F32)


def step_kernel(
    sizes,
    vel_ref, drag_ref, vol_ref, weight_ref, cell_ref, counts_ref, back_hbm,
    pressure_ref, slots_ref,
    back, payload, arrived, total, mom_x, mom_y, mom_z, porous, coef, press,
    vel_t, picked, returned,
    face_xs, face_xr, face_ys, face_yr, face_zs, face_zr,
    back_sem, pay_ssem, pay_rsem, ret_ssem, ret_rsem, halo_ssem, halo_rsem,
):
    n_x, n_y, n_z = sizes
    group = n_y * n_z
    capacity = drag_ref.shape[2]
    size_x, size_y, size_z = pressure_ref.shape
    columns = size_x * size_y
    per_tile = LANES // size_y
    tiles = size_x // per_tile
    at_x, at_y, at_z = lax.axis_index("gx"), lax.axis_index("gy"), lax.axis_index("gz")
    me = at_y * n_z + at_z

    def place(offset):
        there_y = lax.rem(at_y + offset // n_z, n_y)
        there_z = lax.rem(at_z + lax.rem(offset, n_z), n_z)
        return there_y, there_z

    def place_back(offset):
        there_y = lax.rem(at_y - offset // n_z + n_y, n_y)
        there_z = lax.rem(at_z - lax.rem(offset, n_z) + n_z, n_z)
        return there_y, there_z

    x_down = (lax.rem(at_x + n_x - 1, n_x), at_y, at_z)
    x_up = (lax.rem(at_x + 1, n_x), at_y, at_z)
    y_down = (at_x, lax.rem(at_y + n_y - 1, n_y), at_z)
    y_up = (at_x, lax.rem(at_y + 1, n_y), at_z)
    z_down = (at_x, at_y, lax.rem(at_z + n_z - 1, n_z))
    z_up = (at_x, at_y, lax.rem(at_z + 1, n_z))

    barrier = pltpu.get_barrier_semaphore()

    def greet(offset, carry):
        there_y, there_z = place(offset)
        pl.semaphore_signal(barrier, inc=1, device_id=(at_x, there_y, there_z), device_id_type=MESH)
        return carry

    lax.fori_loop(1, group, greet, 0)
    for there in (x_down, x_up):
        pl.semaphore_signal(barrier, inc=1, device_id=there, device_id_type=MESH)

    back_copy = pltpu.make_async_copy(back_hbm, back, back_sem)
    back_copy.start()

    eye = iota((group, group), 0) == iota((group, group), 1)
    counts = jnp.broadcast_to(counts_ref[...].astype(F32), (group, group))
    counts = jnp.sum(jnp.where(eye, counts, 0.0), axis=1, keepdims=True)
    alive = (iota((group, capacity), 1).astype(F32) < counts).astype(F32)
    strength = drag_ref[0] * alive
    cell = cell_ref[0]
    rows = [strength * vel_ref[k, 0] for k in range(3)]
    rows.append(vol_ref[0] * alive)
    rows.append(weight_ref[0])
    rows.append(lax.rem(cell, size_z).astype(F32))
    rows.append(lax.div(cell, size_z).astype(F32))
    for k, row in enumerate(rows):
        payload[:, k, :] = row
    payload[:, 7, :] = rows[6]

    pl.semaphore_wait(barrier, group + 1)

    def payload_copy(offset):
        there_y, there_z = place(offset)
        return pltpu.make_async_remote_copy(
            src_ref=payload.at[there_y * n_z + there_z],
            dst_ref=arrived.at[offset],
            send_sem=pay_ssem.at[offset],
            recv_sem=pay_rsem.at[offset],
            device_id=(at_x, there_y, there_z),
            device_id_type=MESH,
        )

    def send_payload(offset, carry):
        payload_copy(offset).start()
        return carry

    lax.fori_loop(1, group, send_payload, 0)
    arrived[0] = payload[me]
    total[...] = jnp.zeros_like(total)

    width = STEP * capacity

    def chunk_rows(step):
        return jnp.concatenate([arrived[step * STEP + i] for i in range(STEP)], axis=1)

    def column_hot(slots):
        return (iota((columns, width), 0).astype(F32) == slots[6:7]).astype(F32).astype(BF16)

    def deposit(step, carry):
        for i in range(STEP):
            offset = step * STEP + i

            @pl.when(offset > 0)
            def _():
                payload_copy(offset).wait_recv()

        slots = chunk_rows(step)
        hot = column_hot(slots)
        level = iota((size_z, width), 0).astype(F32)
        here = level == slots[5:6]
        above = level == slots[5:6] + 1.0
        share = slots[4:5]
        highs, lows = [], []
        for k in range(4):
            first = split(slots[k : k + 1] * share)
            second = split(slots[k : k + 1] * (1.0 - share))
            for parts, a, b in ((highs, first[0], second[0]), (lows, first[1], second[1])):
                parts.append(jnp.where(here, a, jnp.where(above, b, 0.0)).astype(BF16))
        spread_high = jnp.concatenate(highs, axis=0)
        spread_low = jnp.concatenate(lows, axis=0)
        total[...] += dot(hot, spread_high, ((1,), (1,))) + dot(hot, spread_low, ((1,), (1,)))
        return carry

    lax.fori_loop(0, group // STEP, deposit, 0)

    def halo_copies(exchange, slot, fields):
        copies = []
        for axis, (sends, receives, down, up) in enumerate(
            (
                (face_xs, face_xr, x_down, x_up),
                (face_ys, face_yr, y_down, y_up),
                (face_zs, face_zr, z_down, z_up),
            )
        ):
            for side, there in ((0, down), (1, up)):
                copies.append(
                    pltpu.make_async_remote_copy(
                        src_ref=sends.at[side, pl.ds(slot, fields)],
                        dst_ref=receives.at[1 - side, pl.ds(slot, fields)],
                        send_sem=halo_ssem.at[exchange, 2 * axis + side],
                        recv_sem=halo_rsem.at[exchange, 2 * axis + 1 - side],
                        device_id=there,
                        device_id_type=MESH,
                    )
                )
        return copies

    def start_halos(exchange, slot, fields):
        for copy in halo_copies(exchange, slot, fields):
            copy.start()

    def wait_halos(exchange, slot, fields):
        for copy in halo_copies(exchange, slot, fields):
            copy.wait_recv()

    inside = [
        jnp.where(flag, 1.0, 0.0)
        for flag in (at_x > 0, at_x < n_x - 1, at_y > 0, at_y < n_y - 1, at_z > 0, at_z < n_z - 1)
    ]
    row_of = iota((size_y, size_z), 0)
    lane_of = iota((size_y, size_z), 1)
    diagonals = [lane_of == row_of + j * size_y for j in range(per_tile)]
    first_row, last_row = row_of == 0, row_of == size_y - 1
    first_lane, last_lane = lane_of == 0, lane_of == size_z - 1

    def put_y(slot, x, plane):
        face_ys[0, slot, pl.ds(x, 1), :] = plane[:1]
        face_ys[1, slot, pl.ds(x, 1), :] = plane[size_y - 1 :]

    def put_z(slot, tile, planes):
        for side, lane in ((0, 0), (1, size_z - 1)):
            gathered = 0.0
            for j, plane in enumerate(planes):
                gathered = gathered + jnp.where(diagonals[j], plane[:, lane : lane + 1], 0.0)
            face_zs[side, slot, pl.ds(tile, 1), :] = jnp.sum(gathered, axis=0, keepdims=True)

    def y_low(slot, x):
        return face_yr[0, slot, pl.ds(x, 1), :] * inside[2]

    def y_high(slot, x):
        return face_yr[1, slot, pl.ds(x, 1), :] * inside[3]

    def z_side(side, slot, tile, j):
        row = face_zr[side, slot, pl.ds(tile, 1), :] * inside[4 + side]
        return jnp.sum(jnp.where(diagonals[j], row, 0.0), axis=1, keepdims=True)

    def y_pair(plane, low, high):
        before = jnp.where(first_row, low, pltpu.roll(plane, 1, 0))
        after = jnp.where(last_row, high, pltpu.roll(plane, size_y - 1, 0))
        return before, after

    def z_pair(plane, low, high):
        before = jnp.where(first_lane, low, pltpu.roll(plane, 1, 1))
        after = jnp.where(last_lane, high, pltpu.roll(plane, size_z - 1, 1))
        return before, after

    def tile_rows(tile):
        return pl.ds(pl.multiple_of(tile * LANES, LANES), LANES)

    back_copy.wait()

    def fields_step(tile, carry):
        block = total[tile_rows(tile), :]
        heights = [[], []]
        for j in range(per_tile):
            x = tile * per_tile + j
            part = block[j * size_y : (j + 1) * size_y]
            along = [back[k, x] + part[:, k * size_z : (k + 1) * size_z] for k in range(3)]
            solid = part[:, 3 * size_z :]
            mom_x[x + 1] = along[0]
            mom_y[x] = along[1]
            mom_z[x] = along[2]
            porous[x + 1] = solid
            put_y(0, x, along[1])
            put_y(1, x, solid)
            heights[0].append(along[2])
            heights[1].append(solid)
        put_z(0, tile, heights[0])
        put_z(1, tile, heights[1])
        return carry

    lax.fori_loop(0, tiles, fields_step, 0)
    for side, x in ((0, 1), (1, size_x)):
        face_xs[side, 0] = mom_x[x]
        face_xs[side, 1] = porous[x]
    start_halos(0, 0, 2)

    def porosity_step(tile, carry):
        for j in range(per_tile):
            x = tile * per_tile + j + 1
            porous[x] = 1.0 / (1.0 + porous[x])
        return carry

    lax.fori_loop(0, tiles, porosity_step, 0)
    wait_halos(0, 0, 2)
    for side, x in ((0, 0), (1, size_x + 1)):
        mom_x[x] = face_xr[side, 0] * inside[side]
        porous[x] = 1.0 / (1.0 + face_xr[side, 1] * inside[side])

    def put_pressure(slot, tile, x, planes, buffer):
        for j, plane in enumerate(planes):
            press[buffer, x + j + 1] = plane
            put_y(slot, x + j, plane)
        put_z(slot, tile, planes)

    def send_pressure(exchange, buffer):
        slot = exchange + 1
        for side, x in ((0, 1), (1, size_x)):
            face_xs[side, slot] = press[buffer, x]
        start_halos(exchange, slot, 1)

    def take_pressure(exchange, buffer):
        slot = exchange + 1
        wait_halos(exchange, slot, 1)
        for side, x in ((0, 0), (1, size_x + 1)):
            press[buffer, x] = face_xr[side, slot] * inside[side]

    def weights_step(tile, carry):
        planes = []
        for j in range(per_tile):
            x = tile * per_tile + j
            centre = porous[x + 1]
            around = [porous[x + 2], porous[x]]
            low, high = y_pair(centre, 1.0 / (1.0 + y_low(1, x)), 1.0 / (1.0 + y_high(1, x)))
            around += [high, low]
            low, high = z_pair(
                centre,
                1.0 / (1.0 + z_side(0, 1, tile, j)),
                1.0 / (1.0 + z_side(1, 1, tile, j)),
            )
            around += [high, low]
            faces = [0.5 * (centre + other) for other in around]
            diagonal = faces[0] + faces[1] + faces[2] + faces[3] + faces[4] + faces[5]
            inverse = 1.0 / diagonal
            low, high = y_pair(mom_y[x], y_low(0, x), y_high(0, x))
            source = (mom_x[x + 2] - mom_x[x]) + (high - low)
            low, high = z_pair(mom_z[x], z_side(0, 0, tile, j), z_side(1, 0, tile, j))
            source = 0.5 * (source + (high - low))
            for k in range(6):
                coef[k, x] = faces[k] * inverse
            scaled = source * inverse
            coef[6, x] = scaled
            planes.append(-scaled)
        put_pressure(2, tile, tile * per_tile, planes, 1)
        return carry

    lax.fori_loop(0, tiles, weights_step, 0)
    send_pressure(1, 1)

    def sweep(exchange, carry):
        buffer = lax.rem(exchange, 2)
        take_pressure(exchange, buffer)
        slot = exchange + 1

        def sweep_step(tile, inner):
            planes = []
            for j in range(per_tile):
                x = tile * per_tile + j
                centre = press[buffer, x + 1]
                new = coef[0, x] * press[buffer, x + 2] + coef[1, x] * press[buffer, x]
                low, high = y_pair(centre, y_low(slot, x), y_high(slot, x))
                new = new + coef[2, x] * high + coef[3, x] * low
                low, high = z_pair(
                    centre, z_side(0, slot, tile, j), z_side(1, slot, tile, j)
                )
                new = new + coef[4, x] * high + coef[5, x] * low
                planes.append(new - coef[6, x])
            put_pressure(slot + 1, tile, tile * per_tile, planes, 1 - buffer)
            return inner

        lax.fori_loop(0, tiles, sweep_step, 0)
        send_pressure(exchange + 1, 1 - buffer)
        return carry

    lax.fori_loop(1, SWEEPS, sweep, 0)

    last = SWEEPS % 2
    take_pressure(SWEEPS, last)

    def velocity_step(tile, carry):
        parts = [[], [], []]
        for j in range(per_tile):
            x = tile * per_tile + j
            centre = press[last, x + 1]
            pressure_ref[x] = centre
            hollow = porous[x + 1]
            slope = press[last, x + 2] - press[last, x]
            parts[0].append(hollow * (mom_x[x + 1] - 0.5 * slope))
            low, high = y_pair(centre, y_low(SWEEPS + 1, x), y_high(SWEEPS + 1, x))
            parts[1].append(hollow * (mom_y[x] - 0.5 * (high - low)))
            low, high = z_pair(
                centre, z_side(0, SWEEPS + 1, tile, j), z_side(1, SWEEPS + 1, tile, j)
            )
            parts[2].append(hollow * (mom_z[x] - 0.5 * (high - low)))
        for k in range(3):
            turned = jnp.concatenate(parts[k], axis=0).T
            high, low = split(turned)
            vel_t[k * size_z : (k + 1) * size_z, tile_rows(tile)] = high.astype(BF16)
            vel_t[(3 + k) * size_z : (4 + k) * size_z, tile_rows(tile)] = low.astype(BF16)
        return carry

    lax.fori_loop(0, tiles, velocity_step, 0)

    def return_copy(offset):
        there_y, there_z = place_back(offset)
        return pltpu.make_async_remote_copy(
            src_ref=picked.at[offset],
            dst_ref=returned.at[me],
            send_sem=ret_ssem.at[offset],
            recv_sem=ret_rsem.at[offset],
            device_id=(at_x, there_y, there_z),
            device_id_type=MESH,
        )

    def pick(turn, carry):
        step = group // STEP - 1 - turn
        slots = chunk_rows(step)
        both = dot(vel_t[...], column_hot(slots), ((1,), (0,)))
        level = iota((size_z, width), 0).astype(F32)
        share = slots[4:5]
        reach = jnp.where(
            level == slots[5:6], share, jnp.where(level == slots[5:6] + 1.0, 1.0 - share, 0.0)
        )
        found = []
        for k in range(3):
            value = (
                both[k * size_z : (k + 1) * size_z] + both[(3 + k) * size_z : (4 + k) * size_z]
            )
            found.append(jnp.sum(value * reach, axis=0, keepdims=True))
        found.append(jnp.zeros_like(found[0]))
        found = jnp.concatenate(found, axis=0)
        for i in range(STEP):
            offset = step * STEP + i
            picked[offset] = found[:, i * capacity : (i + 1) * capacity]

            @pl.when(offset > 0)
            def _():
                return_copy(offset).start()

        return carry

    lax.fori_loop(0, group // STEP, pick, 0)
    returned[me] = picked[0]

    def finish(offset, carry):
        copy = return_copy(offset)
        copy.wait_recv()
        copy.wait_send()
        payload_copy(offset).wait_send()
        return carry

    lax.fori_loop(1, group, finish, 0)
    for k in range(3):
        slots_ref[k, 0] = returned[:, k, :] * alive

    def finish_halos(exchange, carry):
        for copy in halo_copies(exchange, exchange + 1, 1):
            copy.wait_send()
        return carry

    for copy in halo_copies(0, 0, 2):
        copy.wait_send()
    lax.fori_loop(1, SWEEPS + 1, finish_halos, 0)


def per_device(sizes, *args):
    vel, drag = args[0], args[1]
    back = args[6]
    group, capacity = drag.shape[1:]
    _, size_x, size_y, size_z = back.shape
    columns = size_x * size_y
    tile_rows = columns // LANES
    slots = SWEEPS + 2
    vmem = pl.BlockSpec(memory_space=pltpu.VMEM)
    field = pltpu.VMEM((size_x, size_y, size_z), F32)
    padded = pltpu.VMEM((size_x + 2, size_y, size_z), F32)
    dma = pltpu.SemaphoreType.DMA
    return pl.pallas_call(
        functools.partial(step_kernel, sizes),
        out_shape=(
            jax.ShapeDtypeStruct((size_x, size_y, size_z), F32),
            jax.ShapeDtypeStruct(vel.shape, F32),
        ),
        in_specs=[vmem] * 6 + [pl.BlockSpec(memory_space=pl.ANY)],
        out_specs=(vmem, vmem),
        scratch_shapes=[
            pltpu.VMEM(back.shape, F32),
            pltpu.VMEM((group, 8, capacity), F32),
            pltpu.VMEM((group, 8, capacity), F32),
            pltpu.VMEM((columns, 4 * size_z), F32),
            padded,
            field,
            field,
            padded,
            pltpu.VMEM((7, size_x, size_y, size_z), F32),
            pltpu.VMEM((2, size_x + 2, size_y, size_z), F32),
            pltpu.VMEM((6 * size_z, columns), BF16),
            pltpu.VMEM((group, 4, capacity), F32),
            pltpu.VMEM((group, 4, capacity), F32),
            pltpu.VMEM((2, slots, size_y, size_z), F32),
            pltpu.VMEM((2, slots, size_y, size_z), F32),
            pltpu.VMEM((2, slots, size_x, size_z), F32),
            pltpu.VMEM((2, slots, size_x, size_z), F32),
            pltpu.VMEM((2, slots, tile_rows, LANES), F32),
            pltpu.VMEM((2, slots, tile_rows, LANES), F32),
            dma,
            dma((group,)),
            dma((group,)),
            dma((group,)),
            dma((group,)),
            dma((SWEEPS + 1, 6)),
            dma((SWEEPS + 1, 6)),
        ],
        compiler_params=pltpu.CompilerParams(
            collective_id=0, has_side_effects=True, vmem_limit_bytes=56 * 2**20
        ),
    )(*args)


def solution(mesh):
    sizes = (mesh.shape["gx"], mesh.shape["gy"], mesh.shape["gz"])
    block = ("gx", "gy", "gz")
    return jax.shard_map(
        functools.partial(per_device, sizes),
        mesh=mesh,
        in_specs=(
            P(None, block, None, None),
            P(block, None, None),
            P(block, None, None),
            P(block, None, None),
            P(block, None, None),
            P(block, None),
            P(None, *block),
        ),
        out_specs=(P(*block), P(None, block, None, None)),
        check_vma=False,
    )
```

time: 297 us -> 90.6 us (0.31)
  the two profiles are of different devices: /device:TPU:129 before, /device:TPU:2 now
where the time goes in v1:
time: 90.6 us; the launch traced here: 90.4 us
  Pallas kernels  86.3 us (95%)
  local copies, waits for them, and re-layouts  3.41 us (4%)
    pallas_call x1, Pallas kernels, per_device(): pl.pallas_call(functools.partial(step_kernel, sizes), out_shape=(jax.Shap...  86.3 us
    unnamed x2, local copies, waits for them, and re-layouts  3.41 us

profile of v1, /device:TPU:2, one launch (start us, length us, event | category | flops | bytes accessed | tf_op | source)
XLA Modules:
  0.0 90.4 jit_solution(17165876592121604088)
XLA Ops:
  0.6 86.3 %shard_map.86 = (f32[32,32,128]{2,1,0:T(8,128)}, f32[3,1,32,256]{3,2,1,0:T(8,128)}) custom-call(f32[3,1,32,256]{3,2,1,0:T(8,128)} %vel_ref.1, f32[1,32,256]{2,1,0:T(8,128)} %drag_ref.1, f32[1,32,256]{2,1,0:T(8,128)} %vol_ref.1, f32[1,32,256]{2,1,0:T(8,128)} %weight_ref.1, s32[1,32,256]{2,1,0:T(8,128)} %cell_ref.1, s32[1,32]{1,0:T(1,128)} %counts_ref.1, ...), custom_call_target="tpu_custom_call" | custom-call | tf_op jit(solution)/shard_map/pallas_call | solution.py:444
  87.0 1.9 %copy.11 = f32[32,32,128]{2,1,0:T(8,128)} copy(f32[32,32,128]{2,1,0:T(8,128)} %get-tuple-element.4) | data formatting | bytes 1048576
  88.8 1.5 %copy.12 = f32[3,1,32,256]{3,2,1,0:T(8,128)} copy(f32[3,1,32,256]{3,2,1,0:T(8,128)} %get-tuple-element.5) | data formatting | bytes 196608

commit v2 on v1

v2 whole, which is shorter than its diff:
```python
import functools

import jax
import jax.numpy as jnp
from jax import lax
from jax.experimental import pallas as pl
from jax.experimental.pallas import tpu as pltpu
from jax.sharding import PartitionSpec as P

SWEEPS = 4
F32 = jnp.float32
BF16 = jnp.bfloat16
MESH = pl.DeviceIdType.MESH
LANES = 128
STEP = 4
UNROLL = 4


def iota(shape, dim):
    return lax.broadcasted_iota(jnp.int32, shape, dim)


def dot(lhs, rhs, contract):
    return lax.dot_general(lhs, rhs, (contract, ((), ())), preferred_element_type=F32)


def split(value):
    high = value.astype(BF16)
    return high.astype(F32), value - high.astype(F32)


def step_kernel(
    sizes,
    vel_ref, drag_ref, vol_ref, weight_ref, cell_ref, counts_ref, back_hbm,
    pressure_ref, slots_ref,
    back, payload, arrived, total, mom_x, mom_y, mom_z, porous, coef, press,
    diagonal, edge_x, edge_y, edge_z, work_z, edge_v, vel_t, picked, returned,
    face_xs, face_xr, face_ys, face_yr, face_zs, face_zr,
    back_sem, pay_ssem, pay_rsem, ret_ssem, ret_rsem, halo_ssem, halo_rsem,
):
    n_x, n_y, n_z = sizes
    group = n_y * n_z
    capacity = drag_ref.shape[2]
    columns, size_z = pressure_ref.shape
    size_y = face_xs.shape[2]
    size_x = columns // size_y
    per_tile = LANES // size_y
    tiles = size_x // per_tile
    at_x, at_y, at_z = lax.axis_index("gx"), lax.axis_index("gy"), lax.axis_index("gz")
    me = at_y * n_z + at_z

    def place(offset):
        there_y = lax.rem(at_y + offset // n_z, n_y)
        there_z = lax.rem(at_z + lax.rem(offset, n_z), n_z)
        return there_y, there_z

    def place_back(offset):
        there_y = lax.rem(at_y - offset // n_z + n_y, n_y)
        there_z = lax.rem(at_z - lax.rem(offset, n_z) + n_z, n_z)
        return there_y, there_z

    x_down = (lax.rem(at_x + n_x - 1, n_x), at_y, at_z)
    x_up = (lax.rem(at_x + 1, n_x), at_y, at_z)
    y_down = (at_x, lax.rem(at_y + n_y - 1, n_y), at_z)
    y_up = (at_x, lax.rem(at_y + 1, n_y), at_z)
    z_down = (at_x, at_y, lax.rem(at_z + n_z - 1, n_z))
    z_up = (at_x, at_y, lax.rem(at_z + 1, n_z))

    barrier = pltpu.get_barrier_semaphore()

    def greet(offset, carry):
        there_y, there_z = place(offset)
        pl.semaphore_signal(barrier, inc=1, device_id=(at_x, there_y, there_z), device_id_type=MESH)
        return carry

    lax.fori_loop(1, group, greet, 0)
    for there in (x_down, x_up):
        pl.semaphore_signal(barrier, inc=1, device_id=there, device_id_type=MESH)

    back_copy = pltpu.make_async_copy(back_hbm, back, back_sem)
    back_copy.start()

    eye = iota((group, group), 0) == iota((group, group), 1)
    counts = jnp.broadcast_to(counts_ref[...].astype(F32), (group, group))
    counts = jnp.sum(jnp.where(eye, counts, 0.0), axis=1, keepdims=True)
    alive = (iota((group, capacity), 1).astype(F32) < counts).astype(F32)
    strength = drag_ref[0] * alive
    cell = cell_ref[0]
    rows = [strength * vel_ref[k, 0] for k in range(3)]
    rows.append(vol_ref[0] * alive)
    rows.append(weight_ref[0])
    rows.append(lax.rem(cell, size_z).astype(F32))
    rows.append(lax.div(cell, size_z).astype(F32))
    for k, row in enumerate(rows):
        payload[:, k, :] = row
    payload[:, 7, :] = rows[6]

    pl.semaphore_wait(barrier, group + 1)

    def payload_copy(offset):
        there_y, there_z = place(offset)
        return pltpu.make_async_remote_copy(
            src_ref=payload.at[there_y * n_z + there_z],
            dst_ref=arrived.at[offset],
            send_sem=pay_ssem.at[offset],
            recv_sem=pay_rsem.at[offset],
            device_id=(at_x, there_y, there_z),
            device_id_type=MESH,
        )

    def send_payload(offset, carry):
        payload_copy(offset).start()
        return carry

    lax.fori_loop(1, group, send_payload, 0)
    arrived[0] = payload[me]
    total[...] = jnp.zeros_like(total)

    width = STEP * capacity

    def chunk_rows(step):
        return jnp.concatenate([arrived[step * STEP + i] for i in range(STEP)], axis=1)

    def column_hot(slots):
        return (iota((columns, width), 0).astype(F32) == slots[6:7]).astype(F32).astype(BF16)

    def deposit(step, carry):
        for i in range(STEP):
            offset = step * STEP + i

            @pl.when(offset > 0)
            def _():
                payload_copy(offset).wait_recv()

        slots = chunk_rows(step)
        hot = column_hot(slots)
        level = iota((size_z, width), 0).astype(F32)
        here = level == slots[5:6]
        above = level == slots[5:6] + 1.0
        share = slots[4:5]
        highs, lows = [], []
        for k in range(4):
            first = split(slots[k : k + 1] * share)
            second = split(slots[k : k + 1] * (1.0 - share))
            for parts, a, b in ((highs, first[0], second[0]), (lows, first[1], second[1])):
                parts.append(jnp.where(here, a, jnp.where(above, b, 0.0)).astype(BF16))
        spread_high = jnp.concatenate(highs, axis=0)
        spread_low = jnp.concatenate(lows, axis=0)
        total[...] += dot(hot, spread_high, ((1,), (1,))) + dot(hot, spread_low, ((1,), (1,)))
        return carry

    lax.fori_loop(0, group // STEP, deposit, 0)

    faces = (
        (face_xs, face_xr, x_down, x_up),
        (face_ys, face_yr, y_down, y_up),
        (face_zs, face_zr, z_down, z_up),
    )

    def halo_copies(exchange, slot, fields, axis):
        sends, receives, down, up = faces[axis]
        return [
            pltpu.make_async_remote_copy(
                src_ref=sends.at[side, pl.ds(slot, fields)],
                dst_ref=receives.at[1 - side, pl.ds(slot, fields)],
                send_sem=halo_ssem.at[exchange, 2 * axis + side],
                recv_sem=halo_rsem.at[exchange, 2 * axis + 1 - side],
                device_id=there,
                device_id_type=MESH,
            )
            for side, there in ((0, down), (1, up))
        ]

    def start_halos(*which):
        for copy in halo_copies(*which):
            copy.start()

    def wait_halos(*which):
        for copy in halo_copies(*which):
            copy.wait_recv()

    inside = [
        jnp.where(flag, 1.0, 0.0)
        for flag in (at_x > 0, at_x < n_x - 1, at_y > 0, at_y < n_y - 1, at_z > 0, at_z < n_z - 1)
    ]
    rows_of = iota((LANES, size_z), 0)
    row_in = lax.rem(rows_of, size_y)
    lane_of = iota((LANES, size_z), 1)
    first_row, last_row = row_in == 0, row_in == size_y - 1
    first_lane, last_lane = lane_of == 0, lane_of == size_z - 1
    first_of_all, last_of_all = rows_of == 0, rows_of == LANES - 1
    ends_x = (pl.ds(0, size_y), pl.ds(columns - size_y, size_y))
    ends_x_pad = (pl.ds(size_y, size_y), pl.ds(columns, size_y))
    ends_y = (pl.ds(0, size_x, stride=size_y), pl.ds(size_y - 1, size_x, stride=size_y))
    ends_y_pad = (
        pl.ds(size_y, size_x, stride=size_y),
        pl.ds(2 * size_y - 1, size_x, stride=size_y),
    )
    signs = (-1.0, 1.0)

    def tile_rows(tile, shift=0):
        return pl.ds(pl.multiple_of(tile * LANES + shift * size_y, size_y), LANES)

    def each_tile(body):
        def step(tile, carry):
            body(tile)
            return carry

        lax.fori_loop(0, tiles, step, 0, unroll=UNROLL)

    def before(value, axis):
        return pltpu.roll(value, 1, axis)

    def after(value, axis):
        return pltpu.roll(value, value.shape[axis] - 1, axis)

    def pack(value):
        turned = value.T
        return turned[:1], turned[size_z - 1 :]

    def unpack(low, high):
        return jnp.where(first_of_all, low, jnp.where(last_of_all, high, 0.0)).T

    def put_z(slot, tile, value):
        for side, row in enumerate(pack(value)):
            face_zs[side, slot, pl.ds(tile, 1), :] = row

    back_copy.wait()

    zero_plane = jnp.zeros((size_y, size_z), F32)
    for rows in (pl.ds(0, size_y), pl.ds(columns + size_y, size_y)):
        mom_x[rows] = zero_plane
        porous[rows] = zero_plane
        press[0, rows] = zero_plane
        press[1, rows] = zero_plane

    def fields_step(tile):
        here = tile_rows(tile)
        along = [back[k, here] + total[here, k * size_z : (k + 1) * size_z] for k in range(3)]
        hollow = 1.0 / (1.0 + total[here, 3 * size_z :])
        mom_x[tile_rows(tile, 1)] = along[0]
        mom_y[here] = along[1]
        mom_z[here] = along[2]
        porous[tile_rows(tile, 1)] = hollow
        put_z(0, tile, along[2])
        put_z(1, tile, hollow)

    each_tile(fields_step)
    for side in range(2):
        face_xs[side, 0] = mom_x[ends_x_pad[side]]
        face_xs[side, 1] = porous[ends_x_pad[side]]
    start_halos(0, 0, 2, 0)
    start_halos(0, 0, 2, 2)
    for side in range(2):
        face_ys[side, 0] = mom_y[ends_y[side]]
        face_ys[side, 1] = porous[ends_y_pad[side]]
    start_halos(0, 0, 2, 1)

    def weights_step(tile):
        here = tile_rows(tile)
        centre = porous[tile_rows(tile, 1)]
        half = 0.5 * centre
        coef[0, here] = half + 0.5 * porous[tile_rows(tile, 2)]
        coef[1, here] = half + 0.5 * porous[tile_rows(tile)]
        whole = coef[0, here] + coef[1, here]
        source = mom_x[tile_rows(tile, 2)] - mom_x[tile_rows(tile)]
        for k, axis, value, last, first in (
            (2, 0, mom_y[here], last_row, first_row),
            (4, 1, mom_z[here], last_lane, first_lane),
        ):
            up = half + 0.5 * after(centre, axis)
            down = half + 0.5 * before(centre, axis)
            coef[k, here] = jnp.where(last, 0.0, up)
            coef[k + 1, here] = jnp.where(first, 0.0, down)
            whole = whole + jnp.where(last, half, up) + jnp.where(first, half, down)
            source = source + jnp.where(last, 0.0, after(value, axis))
            source = source - jnp.where(first, 0.0, before(value, axis))
        coef[6, here] = 0.5 * source
        diagonal[here] = whole

    each_tile(weights_step)

    def outside(side, value):
        return value * inside[side] + (1.0 - inside[side])

    wait_halos(0, 0, 2, 2)
    beyond = [outside(4 + side, face_zr[side, 1]) for side in range(2)]
    for side in range(2):
        edge_z[side] = 0.5 * (face_zs[side, 1] + beyond[side])
        work_z[side] = 0.5 * beyond[side]
        work_z[2 + side] = (0.5 * signs[side]) * inside[4 + side] * face_zr[side, 0]

    def halo_z_step(tile):
        here = tile_rows(tile)
        row = pl.ds(tile, 1)
        diagonal[here] += unpack(work_z[0, row], work_z[1, row])
        coef[6, here] += unpack(work_z[2, row], work_z[3, row])

    each_tile(halo_z_step)
    wait_halos(0, 0, 2, 1)
    for side in range(2):
        value = outside(2 + side, face_yr[side, 1])
        edge_y[side] = 0.5 * (face_ys[side, 1] + value)
        diagonal[ends_y[side]] += 0.5 * value
        source_y = (0.5 * signs[side]) * inside[2 + side] * face_yr[side, 0]
        coef[6, ends_y[side]] += source_y
    wait_halos(0, 0, 2, 0)
    for side in range(2):
        value = outside(side, face_xr[side, 1])
        edge_x[side] = 0.5 * (face_xs[side, 1] + value)
        diagonal[ends_x[side]] += 0.5 * value
        coef[6, ends_x[side]] += (0.5 * signs[side]) * inside[side] * face_xr[side, 0]

    def send_x(exchange, slot, buffer):
        for side in range(2):
            face_xs[side, slot] = press[buffer, ends_x_pad[side]]
        start_halos(exchange, slot, 1, 0)

    def send_y(exchange, slot, buffer):
        for side in range(2):
            face_ys[side, slot] = press[buffer, ends_y_pad[side]]
        start_halos(exchange, slot, 1, 1)

    def first_step(tile):
        here = tile_rows(tile)
        inverse = 1.0 / diagonal[here]
        scaled = coef[6, here] * inverse
        diagonal[here] = inverse
        coef[6, here] = scaled
        press[1, tile_rows(tile, 1)] = -scaled
        put_z(2, tile, -scaled)

    each_tile(first_step)
    send_x(1, 2, 1)
    start_halos(1, 2, 1, 2)
    send_y(1, 2, 1)

    def scale_step(tile):
        here = tile_rows(tile)
        inverse = diagonal[here]
        for k in range(6):
            coef[k, here] *= inverse
        for side, row in enumerate(pack(inverse)):
            work_z[side, pl.ds(tile, 1)] = row

    each_tile(scale_step)
    for side in range(2):
        edge_x[side] *= diagonal[ends_x[side]] * inside[side]
        edge_y[side] *= diagonal[ends_y[side]] * inside[2 + side]
        edge_z[side] *= work_z[side] * inside[4 + side]

    def sweep(exchange, carry):
        old = lax.rem(exchange, 2)
        new = 1 - old
        slot = exchange + 1

        def inner_step(tile):
            here = tile_rows(tile)
            centre = press[old, tile_rows(tile, 1)]
            value = coef[0, here] * press[old, tile_rows(tile, 2)]
            value = value + coef[1, here] * press[old, tile_rows(tile)]
            for k, axis in ((2, 0), (4, 1)):
                value = value + coef[k, here] * after(centre, axis)
                value = value + coef[k + 1, here] * before(centre, axis)
            press[new, tile_rows(tile, 1)] = value - coef[6, here]

        each_tile(inner_step)
        wait_halos(exchange, slot, 1, 2)
        for side in range(2):
            work_z[side] = edge_z[side] * face_zr[side, slot]

        def side_z_step(tile):
            row = pl.ds(tile, 1)
            press[new, tile_rows(tile, 1)] += unpack(work_z[0, row], work_z[1, row])

        each_tile(side_z_step)
        wait_halos(exchange, slot, 1, 1)
        for side in range(2):
            press[new, ends_y_pad[side]] += edge_y[side] * face_yr[side, slot]

        each_tile(lambda tile: put_z(slot + 1, tile, press[new, tile_rows(tile, 1)]))
        wait_halos(exchange, slot, 1, 0)
        for side in range(2):
            press[new, ends_x_pad[side]] += edge_x[side] * face_xr[side, slot]
        send_x(exchange + 1, slot + 1, new)
        for tile in (0, tiles - 1):
            put_z(slot + 1, tile, press[new, tile_rows(tile, 1)])
        start_halos(exchange + 1, slot + 1, 1, 2)
        send_y(exchange + 1, slot + 1, new)
        return carry

    lax.fori_loop(1, SWEEPS, sweep, 0)

    last = SWEEPS % 2
    slot = SWEEPS + 1

    def put_velocity(k, rows, where, value):
        high, low = split(value)
        vel_t[pl.ds(k * size_z + rows.start, rows.size), where] = high.astype(BF16)
        vel_t[pl.ds((3 + k) * size_z + rows.start, rows.size), where] = low.astype(BF16)

    all_z = pl.ds(0, size_z)

    def velocity_step(tile):
        here = tile_rows(tile)
        centre = press[last, tile_rows(tile, 1)]
        pressure_ref[here] = centre
        hollow = porous[tile_rows(tile, 1)]
        slope = press[last, tile_rows(tile, 2)] - press[last, tile_rows(tile)]
        value = hollow * (mom_x[tile_rows(tile, 1)] - 0.5 * slope)
        mom_x[tile_rows(tile, 1)] = value
        put_velocity(0, all_z, here, value.T)
        high = jnp.where(last_row, 0.0, after(centre, 0))
        low = jnp.where(first_row, 0.0, before(centre, 0))
        mom_y[here] = hollow * (mom_y[here] - 0.5 * (high - low))
        high = jnp.where(last_lane, 0.0, after(centre, 1))
        low = jnp.where(first_lane, 0.0, before(centre, 1))
        value = (hollow * (mom_z[here] - 0.5 * (high - low))).T
        put_velocity(2, all_z, here, value)
        edge_v[0, :, here] = value[:16]
        edge_v[1, :, here] = value[size_z - 16 :]

    each_tile(velocity_step)
    wait_halos(SWEEPS, slot, 1, 1)
    for side in range(2):
        mom_y[ends_y[side]] -= (0.5 * signs[side]) * inside[2 + side] * (
            face_ys[side, 1] * face_yr[side, slot]
        )
    each_tile(lambda tile: put_velocity(1, all_z, tile_rows(tile), mom_y[tile_rows(tile)].T))
    wait_halos(SWEEPS, slot, 1, 2)
    for side in range(2):
        work_z[side] = (-0.5 * signs[side]) * inside[4 + side] * (
            face_zs[side, 1] * face_zr[side, slot]
        )
    block_row = iota((16, LANES), 0)
    for side in range(2):
        for tile in range(tiles):
            here = pl.ds(tile * LANES, LANES)
            fix = jnp.where(block_row == 15 * side, work_z[side, tile : tile + 1], 0.0)
            rows = pl.ds((size_z - 16) * side, 16)
            put_velocity(2, rows, here, edge_v[side, :, here] + fix)
    wait_halos(SWEEPS, slot, 1, 0)
    for side in range(2):
        mom_x[ends_x_pad[side]] -= (0.5 * signs[side]) * inside[side] * (
            porous[ends_x_pad[side]] * face_xr[side, slot]
        )
    for tile in (0, tiles - 1):
        put_velocity(0, all_z, pl.ds(tile * LANES, LANES), mom_x[tile_rows(tile, 1)].T)

    def return_copy(offset):
        there_y, there_z = place_back(offset)
        return pltpu.make_async_remote_copy(
            src_ref=picked.at[offset],
            dst_ref=returned.at[me],
            send_sem=ret_ssem.at[offset],
            recv_sem=ret_rsem.at[offset],
            device_id=(at_x, there_y, there_z),
            device_id_type=MESH,
        )

    def pick(turn, carry):
        step = group // STEP - 1 - turn
        slots = chunk_rows(step)
        both = dot(vel_t[...], column_hot(slots), ((1,), (0,)))
        level = iota((size_z, width), 0).astype(F32)
        share = slots[4:5]
        reach = jnp.where(
            level == slots[5:6], share, jnp.where(level == slots[5:6] + 1.0, 1.0 - share, 0.0)
        )
        found = []
        for k in range(3):
            value = (
                both[k * size_z : (k + 1) * size_z] + both[(3 + k) * size_z : (4 + k) * size_z]
            )
            found.append(jnp.sum(value * reach, axis=0, keepdims=True))
        found.append(jnp.zeros_like(found[0]))
        found = jnp.concatenate(found, axis=0)
        for i in range(STEP):
            offset = step * STEP + i
            picked[offset] = found[:, i * capacity : (i + 1) * capacity]

            @pl.when(offset > 0)
            def _():
                return_copy(offset).start()

        return carry

    lax.fori_loop(0, group // STEP, pick, 0)
    returned[me] = picked[0]

    def finish(offset, carry):
        copy = return_copy(offset)
        copy.wait_recv()
        copy.wait_send()
        payload_copy(offset).wait_send()
        return carry

    lax.fori_loop(1, group, finish, 0)
    for k in range(3):
        slots_ref[k, 0] = returned[:, k, :] * alive

    def finish_halos(exchange, carry):
        for axis in range(3):
            for copy in halo_copies(exchange, exchange + 1, 1, axis):
                copy.wait_send()
        return carry

    for axis in range(3):
        for copy in halo_copies(0, 0, 2, axis):
            copy.wait_send()
    lax.fori_loop(1, SWEEPS + 1, finish_halos, 0)


def store_kernel(pressure_ref, slots_ref, pressure_out, slots_out, sems):
    copies = [
        pltpu.make_async_copy(pressure_ref, pressure_out, sems.at[0]),
        pltpu.make_async_copy(slots_ref, slots_out, sems.at[1]),
    ]
    for copy in copies:
        copy.start()
    for copy in copies:
        copy.wait()


def per_device(sizes, *args):
    vel, drag = args[0], args[1]
    back = args[6]
    group, capacity = drag.shape[1:]
    _, size_x, size_y, size_z = back.shape
    columns = size_x * size_y
    tile_rows = columns // LANES
    slots = SWEEPS + 2
    vmem = pl.BlockSpec(memory_space=pltpu.VMEM)
    field = pltpu.VMEM((columns, size_z), F32)
    padded = pltpu.VMEM((columns + 2 * size_y, size_z), F32)
    dma = pltpu.SemaphoreType.DMA
    pressure, slot_velocity = pl.pallas_call(
        functools.partial(step_kernel, sizes),
        out_shape=(
            jax.ShapeDtypeStruct((columns, size_z), F32),
            jax.ShapeDtypeStruct(vel.shape, F32),
        ),
        in_specs=[vmem] * 6 + [pl.BlockSpec(memory_space=pl.ANY)],
        out_specs=(vmem, vmem),
        scratch_shapes=[
            pltpu.VMEM((3, columns, size_z), F32),
            pltpu.VMEM((group, 8, capacity), F32),
            pltpu.VMEM((group, 8, capacity), F32),
            pltpu.VMEM((columns, 4 * size_z), F32),
            padded,
            field,
            field,
            padded,
            pltpu.VMEM((7, columns, size_z), F32),
            pltpu.VMEM((2, columns + 2 * size_y, size_z), F32),
            field,
            pltpu.VMEM((2, size_y, size_z), F32),
            pltpu.VMEM((2, size_x, size_z), F32),
            pltpu.VMEM((2, tile_rows, LANES), F32),
            pltpu.VMEM((4, tile_rows, LANES), F32),
            pltpu.VMEM((2, 16, columns), F32),
            pltpu.VMEM((6 * size_z, columns), BF16),
            pltpu.VMEM((group, 4, capacity), F32),
            pltpu.VMEM((group, 4, capacity), F32),
            pltpu.VMEM((2, slots, size_y, size_z), F32),
            pltpu.VMEM((2, slots, size_y, size_z), F32),
            pltpu.VMEM((2, slots, size_x, size_z), F32),
            pltpu.VMEM((2, slots, size_x, size_z), F32),
            pltpu.VMEM((2, slots, tile_rows, LANES), F32),
            pltpu.VMEM((2, slots, tile_rows, LANES), F32),
            dma,
            dma((group,)),
            dma((group,)),
            dma((group,)),
            dma((group,)),
            dma((SWEEPS + 1, 6)),
            dma((SWEEPS + 1, 6)),
        ],
        compiler_params=pltpu.CompilerParams(
            collective_id=0, has_side_effects=True, vmem_limit_bytes=56 * 2**20
        ),
    )(*args[:6], back.reshape(3, columns, size_z))
    anywhere = pl.BlockSpec(memory_space=pl.ANY)
    pressure, slot_velocity = pl.pallas_call(
        store_kernel,
        out_shape=(
            jax.ShapeDtypeStruct(pressure.shape, F32),
            jax.ShapeDtypeStruct(slot_velocity.shape, F32),
        ),
        in_specs=[vmem, vmem],
        out_specs=(anywhere, anywhere),
        scratch_shapes=[dma((2,))],
    )(pressure, slot_velocity)
    return pressure.reshape(size_x, size_y, size_z), slot_velocity


def solution(mesh):
    sizes = (mesh.shape["gx"], mesh.shape["gy"], mesh.shape["gz"])
    block = ("gx", "gy", "gz")
    return jax.shard_map(
        functools.partial(per_device, sizes),
        mesh=mesh,
        in_specs=(
            P(None, block, None, None),
            P(block, None, None),
            P(block, None, None),
            P(block, None, None),
            P(block, None, None),
            P(block, None),
            P(None, *block),
        ),
        out_specs=(P(*block), P(None, block, None, None)),
        check_vma=False,
    )
```

time: 90.6 us -> 76.2 us (0.84)
  Pallas kernels: 86.3 us -> 75.4 us
  local copies, waits for them, and re-layouts: 3.41 us -> 0 us
    pallas_call x1, Pallas kernels: 86.3 us -> 73.5 us  [per_device(): pl.pallas_call(functools.partial(step_kernel, sizes), out_shape=(jax.Shap...]
    unnamed x2 -> x0, local copies, waits for them, and re-layouts: 3.41 us -> none
    pallas_call x0 -> x1, Pallas kernels: none -> 1.88 us  [per_device(): pl.pallas_call(store_kernel, out_shape=(jax.ShapeDtypeStruct(pressure.sha...]
where the time goes in v2:
time: 76.2 us; the launch traced here: 76.1 us
  Pallas kernels  75.4 us (99%)
    pallas_call x1, Pallas kernels, per_device(): pl.pallas_call(functools.partial(step_kernel, sizes), out_shape=(jax.Shap...  73.5 us
    pallas_call x1, Pallas kernels, per_device(): pl.pallas_call(store_kernel, out_shape=(jax.ShapeDtypeStruct(pressure.sha...  1.88 us

profile of v2, /device:TPU:2, one launch (start us, length us, event | category | flops | bytes accessed | tf_op | source)
XLA Modules:
  0.0 76.1 jit_solution(15542773590985288923)
XLA Ops:
  0.6 73.5 %shard_map.86 = (f32[1024,128]{1,0:T(8,128)}, f32[3,1,32,256]{3,2,1,0:T(8,128)}) custom-call(f32[3,1,32,256]{3,2,1,0:T(8,128)} %vel_ref.1, f32[1,32,256]{2,1,0:T(8,128)} %drag_ref.1, f32[1,32,256]{2,1,0:T(8,128)} %vol_ref.1, f32[1,32,256]{2,1,0:T(8,128)} %weight_ref.1, s32[1,32,256]{2,1,0:T(8,128)} %cell_ref.1, s32[1,32]{1,0:T(1,128)} %counts_ref.1, ...), custom_call_target="tpu_custom_call" | custom-call | tf_op jit(solution)/shard_map/pallas_call | solution.py:537
  74.2 1.9 %shard_map.87 = (f32[1024,128]{1,0:T(8,128)}, f32[3,1,32,256]{3,2,1,0:T(8,128)}) custom-call(f32[1024,128]{1,0:T(8,128)} %get-tuple-element.6.pressure_ref, f32[3,1,32,256]{3,2,1,0:T(8,128)} %get-tuple-element.7.slots_ref), custom_call_target="tpu_custom_call" | custom-call | tf_op jit(solution)/shard_map/pallas_call | solution.py:584
